TPU v7x, 32 devices: a whole 2x2x4 slice. The times are simulated.
32 devices in a mesh: tm: 4 (over y, core), rows: 8 (over z, x).
Axes of the slice: x: 2, y: 2, z: 4, core: 2. Of those that a mesh axis runs over, the one named last changes fastest.
Arguments:
- latent: bfloat16 [8, 32, 16, 384], P('tm', 'rows'), may hold values from -6 to 6
- gain_first: float32 [384], replicated, may hold values from 0.5 to 2
- conv_first: bfloat16 [27, 384, 384], P(None, 'tm'), may hold values from -0.0625 to 0.0625
- bias_first: float32 [384], replicated, may hold values from -0.5 to 0.5
- conv_upper: bfloat16 [9, 384, 192], replicated, may hold values from -0.109375 to 0.109375
- bias_upper: float32 [192], replicated, may hold values from -0.5 to 0.5
Outputs:
- decoded: bfloat16 [8, 64, 6144], P('tm', 'rows')
All inputs are finite; a program needn't handle non-finite values.
Results may differ from a plain program's by a relative error of at most 0.0052.
Values may be sent and summed in bfloat16 or wider, within the bound.
A program may use at most 64 MiB of HBM per device.

v0:
```python
import jax
import jax.numpy as jnp
from jax import lax
from jax.sharding import PartitionSpec as P


def from_behind(block, axis, distance):
    devices = range(lax.axis_size(axis))
    route = [(i - distance, i) for i in devices if i - distance in devices]
    return lax.ppermute(block, axis, route)


def padded_2(shard, sides, width):
    for axis, dim in sides:
        count, length = (lax.axis_size(axis), shard.shape[dim])
        up = [(i, (i + 1) % count) for i in range(count - 1)]
        down = [(j, i) for i, j in up]
        last = lax.slice_in_dim(shard, length - width, length, axis=dim)
        initial = lax.slice_in_dim(shard, 0, width, axis=dim)
        before = lax.ppermute(last, axis, up)
        after = lax.ppermute(initial, axis, down)
        shard = jnp.concatenate([before, shard, after], axis=dim)
    return shard


def scaled_silu(features, gain):
    values = features.astype(jnp.float32)
    mean_square = jnp.mean(values * values, axis=-1, keepdims=True)
    scaled = values * lax.rsqrt(mean_square + 1e-06) * gain
    return (scaled * jax.nn.sigmoid(scaled)).astype(jnp.bfloat16)


def tap_products(padded, weight_piece, frames, rows_out, width):
    count = weight_piece.shape[1]
    outputs = weight_piece.shape[2]
    cells = frames * rows_out * width
    running = jnp.zeros((cells, outputs), jnp.float32)
    for depth_tap in range(3):
        for row_tap in range(3):
            for col_tap in range(3):
                window = padded[
                    depth_tap : depth_tap + frames,
                    row_tap : row_tap + rows_out,
                    col_tap : col_tap + width,
                ]
                part = window.reshape(cells, count)
                running = running + jnp.dot(
                    part,
                    weight_piece[9 * depth_tap + 3 * row_tap + col_tap],
                    preferred_element_type=jnp.float32,
                )
    return running


def causal_conv(activated, kernel, bias):
    frames = activated.shape[0]
    rows_out = activated.shape[1] - 2
    width = activated.shape[2]
    previous = from_behind(activated, "tm", 1)
    stacked = jnp.concatenate([previous, activated], axis=0)
    padded = jnp.pad(stacked, ((0, 0), (0, 0), (1, 1), (0, 0)))
    outputs = kernel.shape[2]
    summed = tap_products(
        padded, lax.all_gather(kernel, "tm", axis=1, tiled=True), frames, rows_out, width
    )
    return (summed + bias).reshape(frames, rows_out, width, outputs)


def local(latent, gain_first, conv_first, bias_first, conv_upper, bias_upper):
    rows_dev = latent.shape[1]
    bordered = padded_2(latent, (("rows", 1),), 1)
    conv_out = causal_conv(scaled_silu(bordered, gain_first), conv_first, bias_first)
    block_out = (latent.astype(jnp.float32) + conv_out).astype(jnp.bfloat16)
    block_bordered = padded_2(block_out, (("rows", 1),), 1)
    frames = block_bordered.shape[0]
    width = block_bordered.shape[2]
    chans = block_bordered.shape[3]
    outputs = conv_upper.shape[2]
    widened = jnp.pad(block_bordered, ((0, 0), (0, 0), (1, 1), (0, 0)))
    larger = jnp.repeat(jnp.repeat(widened, 2, axis=1), 2, axis=2)
    window = larger[:, 1 : 2 * rows_dev + 3, 1 : 2 * width + 3]
    cells = frames * 2 * rows_dev * 2 * width
    result = jnp.zeros((cells, outputs), jnp.float32)
    for row_tap in range(3):
        for col_tap in range(3):
            piece = window[
                :, row_tap : row_tap + 2 * rows_dev, col_tap : col_tap + 2 * width
            ].reshape(cells, chans)
            result = result + jnp.dot(
                piece, conv_upper[3 * row_tap + col_tap], preferred_element_type=jnp.float32
            )
    result = (result + bias_upper).astype(jnp.bfloat16)
    return result.reshape(frames, 2 * rows_dev, 2 * width * outputs)


def solution(mesh):
    in_specs = (P("tm", "rows", None, None), P(), P(None, "tm", None), P(), P(), P())
    out_specs = P("tm", "rows", None)
    return jax.shard_map(local, mesh=mesh, in_specs=in_specs, out_specs=out_specs, check_vma=False)
```

profile of v0, /device:TPU:0, one launch (start us, length us, event | category | flops | bytes accessed | tf_op | source)
XLA Modules:
  0.0 108.5 jit_solution(12366036861776587859)
XLA Ops:
  6.5 0.7 all-gather.2.cloned.1.call-update
  7.3 0.8 fusion.40
  8.0 4.8 %collective-permute-start = (bf16[2,1,16,384]{3,2,1,0:T(8,128)(2,1)S(1)}, bf16[2,1,16,384]{3,2,1,0:T(8,128)(2,1)S(1)}, u32[]{:S(2)}, u32[]{:S(2)}) collective-permute-start(bf16[2,1,16,384]{3,2,1,0:T(8,128)(2,1)S(1)} %get-tuple-element.43), channel_id=1, source_target_pairs={{0,1},{1,2},{2,3},{3,4},{4,5},{5,6},{6,7},{8,9},{9,10},{10,11},{11... | collective-permute-start | bytes 73736 | tf_op jit(solution)/shard_map/ppermute | solution.py:20
  12.9 1.3 %collective-permute-start.1 = (bf16[2,1,16,384]{3,2,1,0:T(8,128)(2,1)S(1)}, bf16[2,1,16,384]{3,2,1,0:T(8,128)(2,1)S(1)}, u32[]{:S(2)}, u32[]{:S(2)}) collective-permute-start(bf16[2,1,16,384]{3,2,1,0:T(8,128)(2,1)S(1)} %get-tuple-element.44), channel_id=1, source_target_pairs={{1,0},{2,1},{3,2},{4,3},{5,4},{6,5},{7,6},{9,8},{10,9},{11,10},{12... | collective-permute-start | bytes 73736 | tf_op jit(solution)/shard_map/ppermute | solution.py:21
  14.2 0.2 collective-permute-done
  14.4 4.2 %collective-permute-done.1 = bf16[2,1,16,384]{3,2,1,0:T(8,128)(2,1)S(1)} collective-permute-done((bf16[2,1,16,384]{3,2,1,0:T(8,128)(2,1)S(1)}, bf16[2,1,16,384]{3,2,1,0:T(8,128)(2,1)S(1)}, u32[]{:S(2)}, u32[]{:S(2)}) %collective-permute-start.1) | collective-permute-done | bytes 24608 | tf_op jit(solution)/shard_map/ppermute | solution.py:21
  18.6 1.0 fusion.5
  19.6 1.1 %fusion.12 = bf16[2,6,16,384]{3,2,1,0:T(8,128)(2,1)S(1)} fusion(f32[384]{0:T(512)} %param.7, f32[2,6,16]{2,1,0:T(8,128)S(1)} %add_rsqrt_fusion, bf16[2,1,16,384]{3,2,1,0:T(8,128)(2,1)S(1)} %collective-permute-done.1, bf16[2,4,16,384]{3,2,1,0:T(8,128)(2,1)} %param.6, bf16[2,1,16,384]{3,2,1,0:T(8,128)(2,1)S(1)} %collective-permute-done), kind=kLoop, calls=%fused_computation.71 | loop fusion | flops 737280 | bytes 297216 | tf_op jit(solution)/shard_map/convert_element_type | solution.py:30
  20.7 1.3 %collective-permute-start.2 = (bf16[2,6,16,384]{3,2,1,0:T(8,128)(2,1)S(1)}, bf16[2,6,16,384]{3,2,1,0:T(8,128)(2,1)S(1)}, u32[]{:S(2)}, u32[]{:S(2)}) collective-permute-start(bf16[2,6,16,384]{3,2,1,0:T(8,128)(2,1)S(1)} %fusion.12), channel_id=1, source_target_pairs={{0,8},{8,16},{16,24},{1,9},{9,17},{17,25},{2,10},{10,18},{18,26},{... | collective-permute-start | bytes 442376 | tf_op jit(solution)/shard_map/ppermute | solution.py:10
  22.0 1.2 %collective-permute-done.2 = bf16[2,6,16,384]{3,2,1,0:T(8,128)(2,1)S(1)} collective-permute-done((bf16[2,6,16,384]{3,2,1,0:T(8,128)(2,1)S(1)}, bf16[2,6,16,384]{3,2,1,0:T(8,128)(2,1)S(1)}, u32[]{:S(2)}, u32[]{:S(2)}) %collective-permute-start.2) | collective-permute-done | bytes 147488 | tf_op jit(solution)/shard_map/ppermute | solution.py:10
  23.3 0.3 pad_slice_fusion
  23.6 0.1 fusion.37
  23.6 43.9 %all-gather.2.cloned.1.call-done = bf16[27,384,384]{2,1,0:T(8,128)(2,1)} async-done(((bf16[27,96,384]{2,1,0:T(8,128)(2,1)}), bf16[27,384,384]{2,1,0:T(8,128)(2,1)}) %all-gather.2.cloned.1.call-update) | async-done | bytes 7962640 | tf_op jit(solution)/shard_map/all_gather | solution.py:64
  67.5 1.3 %fusion.14 = f32[128,384]{1,0:T(8,128)S(1)} fusion(bf16[128,384]{1,0:T(8,128)(2,1)S(1)} %bitcast.212, bf16[27,384,384]{2,1,0:T(8,128)(2,1)} %all-gather.2.cloned.1.call-done), kind=kOutput, calls=%fused_computation.95 | convolution fusion | flops 37748736 | bytes 589824 | tf_op jit(solution)/shard_map/dot_general | solution.py:47
  68.9 1.5 %fusion.13 = f32[128,384]{1,0:T(8,128)S(1)} fusion(bf16[128,384]{1,0:T(8,128)(2,1)S(1)} %bitcast.211, bf16[27,384,384]{2,1,0:T(8,128)(2,1)} %all-gather.2.cloned.1.call-done), kind=kOutput, calls=%fused_computation.91 | convolution fusion | flops 37748736 | bytes 589824 | tf_op jit(solution)/shard_map/dot_general | solution.py:47
  70.3 1.2 %fusion.15 = f32[128,384]{1,0:T(8,128)S(1)} fusion(bf16[128,384]{1,0:T(8,128)(2,1)S(1)} %bitcast.210, bf16[27,384,384]{2,1,0:T(8,128)(2,1)} %all-gather.2.cloned.1.call-done), kind=kOutput, calls=%fused_computation.101 | convolution fusion | flops 37748736 | bytes 589824 | tf_op jit(solution)/shard_map/dot_general | solution.py:47
  71.5 1.2 %convolution_add_fusion.31 = f32[128,384]{1,0:T(8,128)S(1)} fusion(f32[128,384]{1,0:T(8,128)S(1)} %fusion.15, bf16[128,384]{1,0:T(8,128)(2,1)S(1)} %bitcast.219, bf16[27,384,384]{2,1,0:T(8,128)(2,1)} %all-gather.2.cloned.1.call-done), kind=kOutput, calls=%fused_computation.36 | convolution fusion | flops 37797888 | bytes 786432 | tf_op jit(solution)/shard_map/dot_general | solution.py:47
  72.7 1.2 %convolution_add_fusion.30 = f32[128,384]{1,0:T(8,128)S(1)} fusion(f32[128,384]{1,0:T(8,128)S(1)} %convolution_add_fusion.31, bf16[128,384]{1,0:T(8,128)(2,1)S(1)} %bitcast.209, bf16[27,384,384]{2,1,0:T(8,128)(2,1)} %all-gather.2.cloned.1.call-done), kind=kOutput, calls=%fused_computation.35 | convolution fusion | flops 37797888 | bytes 786432 | tf_op jit(solution)/shard_map/dot_general | solution.py:47
  73.9 1.2 %convolution_add_fusion.29 = f32[128,384]{1,0:T(8,128)S(1)} fusion(f32[128,384]{1,0:T(8,128)S(1)} %convolution_add_fusion.30, bf16[128,384]{1,0:T(8,128)(2,1)S(1)} %bitcast.208, bf16[27,384,384]{2,1,0:T(8,128)(2,1)} %all-gather.2.cloned.1.call-done), kind=kOutput, calls=%fused_computation.34 | convolution fusion | flops 37797888 | bytes 786432 | tf_op jit(solution)/shard_map/dot_general | solution.py:47
  75.0 0.0 copy-start.3
  75.1 1.2 %fusion.4 = f32[128,384]{1,0:T(8,128)S(1)} fusion(f32[128,384]{1,0:T(8,128)S(1)} %fusion.14, f32[128,384]{1,0:T(8,128)S(1)} %convolution_add_fusion.29, bf16[128,384]{1,0:T(8,128)(2,1)S(1)} %bitcast.221, bf16[27,384,384]{2,1,0:T(8,128)(2,1)} %all-gather.2.cloned.1.call-done), kind=kOutput, calls=%fused_computation.33 | convolution fusion | flops 37847040 | bytes 983040 | tf_op jit(solution)/shard_map/dot_general | solution.py:47
  76.2 0.0 copy-start.2
  76.3 1.2 %convolution_add_fusion.27 = f32[128,384]{1,0:T(8,128)S(1)} fusion(f32[128,384]{1,0:T(8,128)S(1)} %fusion.4, bf16[128,384]{1,0:T(8,128)(2,1)S(1)} %bitcast.207, bf16[27,384,384]{2,1,0:T(8,128)(2,1)} %all-gather.2.cloned.1.call-done), kind=kOutput, calls=%fused_computation.31 | convolution fusion | flops 37797888 | bytes 786432 | tf_op jit(solution)/shard_map/dot_general | solution.py:47
  77.5 1.2 %fusion.3 = f32[128,384]{1,0:T(8,128)S(1)} fusion(f32[128,384]{1,0:T(8,128)S(1)} %fusion.13, f32[128,384]{1,0:T(8,128)S(1)} %convolution_add_fusion.27, bf16[128,384]{1,0:T(8,128)(2,1)S(1)} %bitcast.220, bf16[27,384,384]{2,1,0:T(8,128)(2,1)} %all-gather.2.cloned.1.call-done), kind=kOutput, calls=%fused_computation.30 | convolution fusion | flops 37847040 | bytes 983040 | tf_op jit(solution)/shard_map/dot_general | solution.py:47
  78.6 1.2 %convolution_add_fusion.25 = f32[128,384]{1,0:T(8,128)S(1)} fusion(f32[128,384]{1,0:T(8,128)S(1)} %fusion.3, bf16[128,384]{1,0:T(8,128)(2,1)S(1)} %bitcast.206, bf16[27,384,384]{2,1,0:T(8,128)(2,1)} %all-gather.2.cloned.1.call-done), kind=kOutput, calls=%fused_computation.28 | convolution fusion | flops 37797888 | bytes 786432 | tf_op jit(solution)/shard_map/dot_general | solution.py:47
  79.8 1.2 %convolution_add_fusion.24 = f32[128,384]{1,0:T(8,128)S(1)} fusion(f32[128,384]{1,0:T(8,128)S(1)} %convolution_add_fusion.25, bf16[128,384]{1,0:T(8,128)(2,1)S(1)} %bitcast.218, bf16[27,384,384]{2,1,0:T(8,128)(2,1)} %all-gather.2.cloned.1.call-done), kind=kOutput, calls=%fused_computation.27 | convolution fusion | flops 37797888 | bytes 786432 | tf_op jit(solution)/shard_map/dot_general | solution.py:47
  81.0 0.2 convolution_add_fusion.23
  81.2 0.2 convolution_add_fusion.22
  81.4 0.2 convolution_add_fusion.21
  81.7 0.2 convolution_add_fusion.20
  81.9 0.2 convolution_add_fusion.19
  82.1 0.2 convolution_add_fusion.18
  82.3 0.2 convolution_add_fusion.17
  82.5 0.2 convolution_add_fusion.16
  82.8 0.2 convolution_add_fusion.15
  83.0 0.2 convolution_add_fusion.14
  83.2 0.2 convolution_add_fusion.13
  83.4 0.2 convolution_add_fusion.12
  83.6 0.2 convolution_add_fusion.11
  83.9 0.2 convolution_add_fusion.10
  84.1 0.2 convolution_add_fusion.9
  84.3 0.2 fusion.2
  84.6 3.4 %collective-permute-start.3 = (bf16[2,1,16,384]{3,2,1,0:T(8,128)(2,1)S(1)}, bf16[2,1,16,384]{3,2,1,0:T(8,128)(2,1)S(1)}, u32[]{:S(2)}, u32[]{:S(2)}) collective-permute-start(bf16[2,1,16,384]{3,2,1,0:T(8,128)(2,1)S(1)} %get-tuple-element.41), channel_id=1, source_target_pairs={{0,1},{1,2},{2,3},{3,4},{4,5},{5,6},{6,7},{8,9},{9,10},{10,11},{11... | collective-permute-start | bytes 73736 | tf_op jit(solution)/shard_map/ppermute | solution.py:20
  87.9 1.3 %collective-permute-start.4 = (bf16[2,1,16,384]{3,2,1,0:T(8,128)(2,1)S(1)}, bf16[2,1,16,384]{3,2,1,0:T(8,128)(2,1)S(1)}, u32[]{:S(2)}, u32[]{:S(2)}) collective-permute-start(bf16[2,1,16,384]{3,2,1,0:T(8,128)(2,1)S(1)} %get-tuple-element.42), channel_id=1, source_target_pairs={{1,0},{2,1},{3,2},{4,3},{5,4},{6,5},{7,6},{9,8},{10,9},{11,10},{12... | collective-permute-start | bytes 73736 | tf_op jit(solution)/shard_map/ppermute | solution.py:21
  89.2 0.2 collective-permute-done.3
  89.4 4.2 %collective-permute-done.4 = bf16[2,1,16,384]{3,2,1,0:T(8,128)(2,1)S(1)} collective-permute-done((bf16[2,1,16,384]{3,2,1,0:T(8,128)(2,1)S(1)}, bf16[2,1,16,384]{3,2,1,0:T(8,128)(2,1)S(1)}, u32[]{:S(2)}, u32[]{:S(2)}) %collective-permute-start.4) | collective-permute-done | bytes 24608 | tf_op jit(solution)/shard_map/ppermute | solution.py:21
  93.7 0.1 copy.20
  93.8 0.0 copy-start.1
  93.8 0.1 pad.9.clone
  94.0 0.2 broadcast_in_dim.4
  94.1 0.3 broadcast_in_dim.5
  94.5 2.8 %fusion.38 = (bf16[2,8,32,384]{3,0,2,1:T(2,128)(2,1)S(1)}, bf16[2,8,32,384]{3,0,2,1:T(2,128)(2,1)S(1)}, bf16[2,8,32,384]{3,0,2,1:T(2,128)(2,1)S(1)}, bf16[2,8,32...) fusion(bf16[2,12,36,384]{3,0,2,1:T(2,128)(2,1)S(1)} %bitcast.183), kind=kLoop, calls=%fused_computation.128 | loop fusion | bytes 7077888 | tf_op jit(solution)/shard_map/slice | solution.py:86
  97.4 0.0 copy-start.4
  97.8 0.3 fusion.24
  98.1 0.3 convolution_add_fusion.7
  98.4 0.3 convolution_add_fusion.6
  98.7 0.3 convolution_add_fusion.5
  99.0 0.3 convolution_add_fusion.4
  99.3 0.3 convolution_add_fusion.3
  99.6 0.3 convolution_add_fusion.2
  99.9 0.3 convolution_add_fusion.1
  100.3 0.3 fusion.1
  100.6 0.1 copy.19
  100.7 0.9 reshape.170
  (21 shorter events, 0.5 us)
Async XLA Ops:
  6.5 61.0 %all-gather.2.cloned.1.call-start = ((), (), s32[]{:S(2)}) async-start(), calls=%async_computation | async-start | bytes 9953280 | tf_op jit(solution)/shard_map/all_gather | solution.py:64
  8.0 6.3 %collective-permute-start = (bf16[2,1,16,384]{3,2,1,0:T(8,128)(2,1)S(1)}, bf16[2,1,16,384]{3,2,1,0:T(8,128)(2,1)S(1)}, u32[]{:S(2)}, u32[]{:S(2)}) collective-permute-start(bf16[2,1,16,384]{3,2,1,0:T(8,128)(2,1)S(1)} %get-tuple-element.43), channel_id=1, source_target_pairs={{0,1},{1,2},{2,3},{3,4},{4,5},{5,6},{6,7},{8,9},{9,10},{10,11},{11... | collective-permute-start | bytes 73736 | tf_op jit(solution)/shard_map/ppermute | solution.py:20
  12.9 5.7 %collective-permute-start.1 = (bf16[2,1,16,384]{3,2,1,0:T(8,128)(2,1)S(1)}, bf16[2,1,16,384]{3,2,1,0:T(8,128)(2,1)S(1)}, u32[]{:S(2)}, u32[]{:S(2)}) collective-permute-start(bf16[2,1,16,384]{3,2,1,0:T(8,128)(2,1)S(1)} %get-tuple-element.44), channel_id=1, source_target_pairs={{1,0},{2,1},{3,2},{4,3},{5,4},{6,5},{7,6},{9,8},{10,9},{11,10},{12... | collective-permute-start | bytes 73736 | tf_op jit(solution)/shard_map/ppermute | solution.py:21
  20.7 2.5 %collective-permute-start.2 = (bf16[2,6,16,384]{3,2,1,0:T(8,128)(2,1)S(1)}, bf16[2,6,16,384]{3,2,1,0:T(8,128)(2,1)S(1)}, u32[]{:S(2)}, u32[]{:S(2)}) collective-permute-start(bf16[2,6,16,384]{3,2,1,0:T(8,128)(2,1)S(1)} %fusion.12), channel_id=1, source_target_pairs={{0,8},{8,16},{16,24},{1,9},{9,17},{17,25},{2,10},{10,18},{18,26},{... | collective-permute-start | bytes 442376 | tf_op jit(solution)/shard_map/ppermute | solution.py:10
  67.5 13.5 %copy-start = (bf16[27,384,384]{2,1,0:T(8,128)(2,1)S(1)}, bf16[27,384,384]{2,1,0:T(8,128)(2,1)}, u32[]{:S(2)}) copy-start(bf16[27,384,384]{2,1,0:T(8,128)(2,1)} %all-gather.2.cloned.1.call-done) | copy-start | bytes 23887876
  75.0 9.3 %copy-start.3 = (f32[384]{0:T(512)S(1)}, f32[384]{0:T(512)}, u32[]{:S(2)}) copy-start(f32[384]{0:T(512)} %param.9) | copy-start | bytes 4612
  76.2 8.3 %copy-start.2 = (bf16[2,4,16,384]{3,2,1,0:T(8,128)(2,1)S(1)}, bf16[2,4,16,384]{3,2,1,0:T(8,128)(2,1)}, u32[]{:S(2)}) copy-start(bf16[2,4,16,384]{3,2,1,0:T(8,128)(2,1)} %param.6) | copy-start | bytes 294916
  84.6 4.9 %collective-permute-start.3 = (bf16[2,1,16,384]{3,2,1,0:T(8,128)(2,1)S(1)}, bf16[2,1,16,384]{3,2,1,0:T(8,128)(2,1)S(1)}, u32[]{:S(2)}, u32[]{:S(2)}) collective-permute-start(bf16[2,1,16,384]{3,2,1,0:T(8,128)(2,1)S(1)} %get-tuple-element.41), channel_id=1, source_target_pairs={{0,1},{1,2},{2,3},{3,4},{4,5},{5,6},{6,7},{8,9},{9,10},{10,11},{11... | collective-permute-start | bytes 73736 | tf_op jit(solution)/shard_map/ppermute | solution.py:20
  87.9 5.7 %collective-permute-start.4 = (bf16[2,1,16,384]{3,2,1,0:T(8,128)(2,1)S(1)}, bf16[2,1,16,384]{3,2,1,0:T(8,128)(2,1)S(1)}, u32[]{:S(2)}, u32[]{:S(2)}) collective-permute-start(bf16[2,1,16,384]{3,2,1,0:T(8,128)(2,1)S(1)} %get-tuple-element.42), channel_id=1, source_target_pairs={{1,0},{2,1},{3,2},{4,3},{5,4},{6,5},{7,6},{9,8},{10,9},{11,10},{12... | collective-permute-start | bytes 73736 | tf_op jit(solution)/shard_map/ppermute | solution.py:21
  93.8 4.0 %copy-start.1 = (bf16[9,384,192]{1,2,0:T(8,128)(2,1)S(1)}, bf16[9,384,192]{1,2,0:T(8,128)(2,1)}, u32[]{:S(2)}) copy-start(bf16[9,384,192]{1,2,0:T(8,128)(2,1)} %param.10) | copy-start | bytes 3981316
  97.4 2.8 %copy-start.4 = (f32[192]{0:T(256)S(1)}, f32[192]{0:T(256)}, u32[]{:S(2)}) copy-start(f32[192]{0:T(256)} %param.11) | copy-start | bytes 2308
Sparse Core Ops, SparseCore 0:
  8.9 58.5 all-gather.1
where the time goes:
time: 109 us; the launch traced here: 108 us
  waiting for transfers between devices  54.6 us (50%)
  matrix products  19.4 us (18%)
  between operations  14 us (13%)
  starting transfers between devices  12.1 us (11%)
  local copies, waits for them, and re-layouts  6.13 us (6%)
  other arithmetic  2.3 us (2%)
    all_gather x1, waiting for transfers between devices, causal_conv(): lax.all_gather(kernel, 'tm', axis=1, tiled=True)  43.9 us
    dot_general x27, matrix products, tap_products(): jnp.dot(part, weight_piece[9 * depth_tap + 3 * row_tap + col_tap], prefer...  16.7 us
    ppermute x2, waiting for transfers between devices, padded_2(): after = lax.ppermute(initial, axis, down)  8.44 us
    ppermute x2, starting transfers between devices, padded_2(): before = lax.ppermute(last, axis, up)  8.19 us
    slice x10, local copies, waits for them, and re-layouts, local(): window[:, row_tap:row_tap + 2 * rows_dev, col_tap:col_tap + 2 * width]  3.22 us
    dot_general x9, matrix products, local(): jnp.dot(piece, conv_upper[3 * row_tap + col_tap], preferred_element_type=...  2.67 us
    ppermute x2, starting transfers between devices, padded_2(): after = lax.ppermute(initial, axis, down)  2.58 us
  transfers between devices with their start and end apart: 6, of which 6 were waited for; matrix products, arithmetic and copies ran while one was open for 3% of the time, Pallas kernels for 0%

commit v1 on v0

v1 whole, which is shorter than its diff:
```python
import functools

import jax
import jax.numpy as jnp
from jax import lax
from jax.experimental import pallas as pl
from jax.experimental.pallas import tpu as pltpu
from jax.sharding import PartitionSpec as P

MESH = pl.DeviceIdType.MESH
F32 = jnp.float32
BF16 = jnp.bfloat16
LANES = 128


def kernel(
    n_tm,
    n_rows,
    latent_ref,
    small_ref,
    w1_hbm,
    wu_hbm,
    out_ref,
    w1_ref,
    wpad,
    wu_ref,
    send,
    recv,
    shifted,
    part_send,
    part_recv,
    own,
    block,
    pick,
    load_sem,
    act_send_sem,
    act_recv_sem,
    part_send_sem,
    part_recv_sem,
    row_send_sem,
    row_recv_sem,
):
    frames, rows, width, chans = latent_ref.shape
    cells = frames * rows * width
    taps, piece, _ = w1_ref.shape
    outputs = wu_ref.shape[1]
    me = lax.axis_index("tm")
    band = lax.axis_index("rows")
    above = lax.rem(band + n_rows - 1, n_rows)
    below = lax.rem(band + 1, n_rows)
    has_above = band > 0
    has_below = band < n_rows - 1

    load_w1 = pltpu.make_async_copy(w1_hbm, w1_ref, load_sem.at[0])
    load_w1.start()
    load_wu = pltpu.make_async_copy(wu_hbm, wu_ref, load_sem.at[1])
    load_wu.start()

    barrier = pltpu.get_barrier_semaphore()
    for d in range(1, n_tm):
        pl.semaphore_signal(
            barrier, inc=1, device_id=(lax.rem(me + d, n_tm), band), device_id_type=MESH
        )

    @pl.when(has_above)
    def _():
        for s in range(n_tm):
            pl.semaphore_signal(barrier, inc=1, device_id=(s, above), device_id_type=MESH)

    @pl.when(has_below)
    def _():
        for s in range(n_tm):
            pl.semaphore_signal(barrier, inc=1, device_id=(s, below), device_id_type=MESH)

    values = latent_ref[...].astype(F32).reshape(cells, chans)
    mean_square = jnp.mean(values * values, axis=-1, keepdims=True)
    scaled = values * lax.rsqrt(mean_square + 1e-06) * small_ref[pl.ds(0, 1)]
    act = scaled / (1.0 + jnp.exp(-scaled))
    blank = jnp.zeros((cells, LANES - piece), F32)
    for s in range(n_tm):
        cut = jnp.concatenate([act[:, s * piece : (s + 1) * piece], blank], axis=1)
        send[s] = cut.astype(BF16).reshape(frames, rows, width, LANES)

    neighbours = jnp.where(has_above, n_tm, 0) + jnp.where(has_below, n_tm, 0)
    pl.semaphore_wait(barrier, n_tm - 1 + neighbours)

    mine = pl.ds(me * frames, frames)

    def act_copy(s, kind, row, where, to):
        return pltpu.make_async_remote_copy(
            src_ref=send.at[s, :, row],
            dst_ref=recv.at[mine, where],
            send_sem=act_send_sem.at[3 * s + kind],
            recv_sem=act_recv_sem.at[3 * me + kind],
            device_id=(s, to),
            device_id_type=MESH,
        )

    def main_copy(s):
        return act_copy(s, 0, pl.ds(0, rows), pl.ds(1, rows), band)

    def down_copy(s):
        return act_copy(s, 1, pl.ds(rows - 1, 1), pl.ds(0, 1), below)

    def up_copy(s):
        return act_copy(s, 2, pl.ds(0, 1), pl.ds(rows + 1, 1), above)

    for d in range(1, n_tm):
        main_copy(lax.rem(me + d, n_tm)).start()

    @pl.when(has_below)
    def _():
        for s in range(n_tm):
            down_copy(s).start()

    @pl.when(has_above)
    def _():
        for s in range(n_tm):
            up_copy(s).start()

    recv[mine, pl.ds(1, rows)] = send[me]
    all_frames = n_tm * frames
    edge = jnp.zeros((all_frames, 1, width, LANES), BF16)
    block_edge = jnp.zeros((frames, 1, width, chans), BF16)

    @pl.when(band == 0)
    def _():
        recv[:, pl.ds(0, 1)] = edge
        block[:, pl.ds(0, 1)] = block_edge

    @pl.when(band == n_rows - 1)
    def _():
        recv[:, pl.ds(rows + 1, 1)] = edge
        block[:, pl.ds(rows + 1, 1)] = block_edge

    shifted[:, pl.ds(0, 2)] = jnp.zeros((3, 2, rows + 2, width, LANES), BF16)

    big = 2 * rows
    depth = block.shape[1]
    block[:, pl.ds(rows + 2, depth - rows - 2)] = jnp.zeros(
        (frames, depth - rows - 2, width, chans), BF16
    )
    at = lax.broadcasted_iota(jnp.int32, (pick.shape[0], 1), 0)
    to = lax.broadcasted_iota(jnp.int32, pick.shape, 1)
    row_tap = at // (frames * width * big)
    col = (at // (frames * big)) % width
    frame = (at // big) % frames
    line = at % big
    source = frame * (depth * width) + ((line + row_tap + 1) // 2) * width + col
    pick[...] = jnp.where(to == source, 1.0, 0.0).astype(BF16)

    load_w1.wait()
    spare = jnp.zeros((LANES - piece, chans), BF16)
    for tap in range(taps):
        wpad[pl.ds(tap * LANES, LANES)] = jnp.concatenate([w1_ref[tap], spare], axis=0)

    def act_arrival(s, kind, row, where):
        return pltpu.make_async_remote_copy(
            src_ref=send.at[s, :, row],
            dst_ref=recv.at[pl.ds(s * frames, frames), where],
            send_sem=act_send_sem.at[3 * s + kind],
            recv_sem=act_recv_sem.at[3 * s + kind],
            device_id=(lax.rem(me + 1, n_tm), band),
            device_id_type=MESH,
        )

    for d in range(1, n_tm):
        s = lax.rem(me + d, n_tm)
        act_arrival(s, 0, pl.ds(0, rows), pl.ds(1, rows)).wait_recv()

    @pl.when(has_above)
    def _():
        for s in range(n_tm):
            act_arrival(s, 1, pl.ds(0, 1), pl.ds(0, 1)).wait_recv()

    @pl.when(has_below)
    def _():
        for s in range(n_tm):
            act_arrival(s, 2, pl.ds(0, 1), pl.ds(rows + 1, 1)).wait_recv()

    tall = all_frames * (rows + 2) * width
    flat = recv[...].astype(F32).reshape(tall, LANES)
    column = lax.broadcasted_iota(jnp.int32, (tall, LANES), 0) % width
    left = jnp.where(column == 0, 0.0, pltpu.roll(flat, 1, 0))
    right = jnp.where(column == width - 1, 0.0, pltpu.roll(flat, tall - 1, 0))
    shape = (all_frames, rows + 2, width, LANES)
    shifted[0, pl.ds(2, all_frames)] = left.astype(BF16).reshape(shape)
    shifted[1, pl.ds(2, all_frames)] = recv[...]
    shifted[2, pl.ds(2, all_frames)] = right.astype(BF16).reshape(shape)

    pairs = n_tm // 2

    def part_copy(s):
        return pltpu.make_async_remote_copy(
            src_ref=part_send.at[s],
            dst_ref=part_recv.at[me],
            send_sem=part_send_sem.at[s],
            recv_sem=part_recv_sem.at[me],
            device_id=(s, band),
            device_id_type=MESH,
        )

    for k in range(1, pairs + 1):
        pair = lax.rem(lax.div(me, 2) + k, pairs)
        total = jnp.zeros((2 * cells, chans), F32)
        for dt in range(3):
            windows = []
            for dy in range(3):
                for dx in range(3):
                    start = pair * (2 * frames) + dt
                    view = shifted[dx, pl.ds(start, 2 * frames), pl.ds(dy, rows)]
                    windows.append(view.reshape(2 * cells, LANES))
            total = total + jnp.dot(
                jnp.concatenate(windows, axis=1),
                wpad[pl.ds(dt * 9 * LANES, 9 * LANES)],
                preferred_element_type=F32,
            )
        if k < pairs:
            for c in range(2):
                part_send[2 * pair + c] = total[c * cells : (c + 1) * cells].astype(BF16)
                part_copy(2 * pair + c).start()
        else:
            own[...] = total.reshape(2, cells, chans)
            mate = 2 * lax.div(me, 2) + (1 - lax.rem(me, 2))
            part_send[mate] = own[1 - lax.rem(me, 2)].astype(BF16)
            part_copy(mate).start()

    summed = own[lax.rem(me, 2)] + small_ref[pl.ds(8, 1)]
    summed = summed + latent_ref[...].astype(F32).reshape(cells, chans)
    for d in range(1, n_tm):
        s = lax.rem(me + n_tm - d, n_tm)
        pltpu.make_async_remote_copy(
            src_ref=part_send.at[s],
            dst_ref=part_recv.at[s],
            send_sem=part_send_sem.at[s],
            recv_sem=part_recv_sem.at[s],
            device_id=(s, band),
            device_id_type=MESH,
        ).wait_recv()
        summed = summed + part_recv[s].astype(F32)
    block[:, pl.ds(1, rows)] = summed.astype(BF16).reshape(frames, rows, width, chans)

    def row_copy(kind, row, where, to):
        return pltpu.make_async_remote_copy(
            src_ref=block.at[:, pl.ds(row, 1)],
            dst_ref=block.at[:, pl.ds(where, 1)],
            send_sem=row_send_sem.at[kind],
            recv_sem=row_recv_sem.at[kind],
            device_id=(me, to),
            device_id_type=MESH,
        )

    @pl.when(has_below)
    def _():
        row_copy(0, rows, 0, below).start()

    @pl.when(has_above)
    def _():
        row_copy(1, 1, rows + 1, above).start()

    load_wu.wait()

    @pl.when(has_above)
    def _():
        row_copy(0, rows, 0, above).wait_recv()

    @pl.when(has_below)
    def _():
        row_copy(1, 1, rows + 1, below).wait_recv()

    spread = jnp.dot(
        pick[...],
        block[...].reshape(frames * depth * width, chans),
        preferred_element_type=F32,
    ).astype(BF16)
    high = frames * width * big
    lines = jnp.concatenate([spread[k * high : (k + 1) * high] for k in range(3)], axis=1)
    cols = []
    for dx in range(3):
        weights = jnp.concatenate([wu_ref[dx], wu_ref[3 + dx], wu_ref[6 + dx]], axis=1)
        product = lax.dot_general(
            lines, weights, (((1,), (1,)), ((), ())), preferred_element_type=F32
        )
        cols.append(product.reshape(width, frames * big, outputs))
    nothing = jnp.zeros((1, frames * big, outputs), F32)
    before = jnp.concatenate([nothing, cols[0][: width - 1]], axis=0)
    after = jnp.concatenate([cols[2][1:], nothing], axis=0)
    bias2 = small_ref[pl.ds(16, 1)].reshape(1, 1, 2 * outputs)
    even = before + cols[1] + cols[2]
    odd = cols[0] + cols[1] + after
    both = (jnp.concatenate([even, odd], axis=-1) + bias2).astype(BF16)
    for c in range(width):
        out_ref[:, pl.ds(c * 2 * outputs, 2 * outputs)] = both[c]

    for d in range(1, n_tm):
        s = lax.rem(me + d, n_tm)
        main_copy(s).wait_send()
        part_copy(s).wait_send()

    @pl.when(has_below)
    def _():
        for s in range(n_tm):
            down_copy(s).wait_send()
        row_copy(0, rows, 0, below).wait_send()

    @pl.when(has_above)
    def _():
        for s in range(n_tm):
            up_copy(s).wait_send()
        row_copy(1, 1, rows + 1, above).wait_send()


def local(n_tm, n_rows, latent, gain_first, conv_first, bias_first, conv_upper, bias_upper):
    frames, rows, width, chans = latent.shape
    outputs = conv_upper.shape[2]
    taps, piece, _ = conv_first.shape
    cells = frames * rows * width
    all_frames = n_tm * frames
    depth = rows + 4
    vmem = pl.BlockSpec(memory_space=pltpu.VMEM)
    hbm = pl.BlockSpec(memory_space=pl.ANY)
    dma = pltpu.SemaphoreType.DMA
    flops = 2 * taps * piece * chans * all_frames * rows * width + 18 * 4 * cells * chans * outputs
    both_biases = jnp.concatenate([bias_upper, bias_upper])
    small = jnp.concatenate(
        [
            jnp.broadcast_to(row.reshape(1, 2 * outputs), (8, 2 * outputs))
            for row in (gain_first, bias_first, both_biases)
        ]
    )
    decoded = pl.pallas_call(
        functools.partial(kernel, n_tm, n_rows),
        out_shape=jax.ShapeDtypeStruct((frames * 2 * rows, 2 * width * outputs), BF16),
        in_specs=[vmem, vmem, hbm, hbm],
        out_specs=vmem,
        scratch_shapes=[
            pltpu.VMEM(conv_first.shape, BF16),
            pltpu.VMEM((taps * LANES, chans), BF16),
            pltpu.VMEM((9, outputs, chans), BF16),
            pltpu.VMEM((n_tm, frames, rows, width, LANES), BF16),
            pltpu.VMEM((all_frames, rows + 2, width, LANES), BF16),
            pltpu.VMEM((3, all_frames + 2, rows + 2, width, LANES), BF16),
            pltpu.VMEM((n_tm, cells, chans), BF16),
            pltpu.VMEM((n_tm, cells, chans), BF16),
            pltpu.VMEM((2, cells, chans), F32),
            pltpu.VMEM((frames, depth, width, chans), BF16),
            pltpu.VMEM((6 * cells, frames * depth * width), BF16),
            dma((2,)),
            dma((3 * n_tm,)),
            dma((3 * n_tm,)),
            dma((n_tm,)),
            dma((n_tm,)),
            dma((2,)),
            dma((2,)),
        ],
        compiler_params=pltpu.CompilerParams(
            collective_id=0, has_side_effects=True, vmem_limit_bytes=60 * 1024 * 1024
        ),
        cost_estimate=pl.CostEstimate(
            flops=flops, bytes_accessed=4 * 1024 * 1024, transcendentals=cells * chans
        ),
    )(
        latent,
        small,
        conv_first,
        jnp.swapaxes(conv_upper, 1, 2),
    )
    return decoded.reshape(frames, 2 * rows, 2 * width * outputs)


def solution(mesh):
    in_specs = (P("tm", "rows", None, None), P(), P(None, "tm", None), P(), P(), P())
    out_specs = P("tm", "rows", None)
    body = functools.partial(local, mesh.shape["tm"], mesh.shape["rows"])
    return jax.shard_map(body, mesh=mesh, in_specs=in_specs, out_specs=out_specs, check_vma=False)
```

time: 109 us -> 24.7 us (0.23)
  waiting for transfers between devices: 54.6 us -> 0 us
  Pallas kernels: 0 us -> 19.8 us
  matrix products: 19.4 us -> 0 us
  between operations: 14 us -> 0.01 us
  starting transfers between devices: 12.1 us -> 0 us
  local copies, waits for them, and re-layouts: 6.13 us -> 2.99 us
    all_gather x1 -> x0, waiting for transfers between devices: 43.9 us -> none  [causal_conv(): lax.all_gather(kernel, 'tm', axis=1, tiled=True)]
    pallas_call x0 -> x1, Pallas kernels: none -> 19.8 us  [local(): pl.pallas_call(functools.partial(kernel, n_tm, n_rows), out_shape=jax.Sha...]
    dot_general x36 -> x0, matrix products: 19.4 us -> none  [the longest x27 16.7 us: tap_products(): jnp.dot(part, weight_piece[9 * depth_tap + 3 * row_tap + col_tap], prefer...]
    ppermute x5 -> x0, starting transfers between devices: 12.1 us -> none  [the longest x2 8.19 us: padded_2(): before = lax.ppermute(last, axis, up)]
    ppermute x5 -> x0, waiting for transfers between devices: 10 us -> none  [the longest x2 8.44 us: padded_2(): after = lax.ppermute(initial, axis, down)]
    slice x13 -> x0, local copies, waits for them, and re-layouts: 4.28 us -> none  [the longest x10 3.22 us: local(): window[:, row_tap:row_tap + 2 * rows_dev, col_tap:col_tap + 2 * width]]
    unnamed x11 -> x1, local copies, waits for them, and re-layouts: 0.14 us -> 1.62 us
    concatenate x3 -> x2, other arithmetic: 0.14 us -> 1.45 us  [the longest x1 0.83 us: local(): both_biases = jnp.concatenate([bias_upper, bias_upper])]
  transfers between devices with their start and end apart: 6 -> 0, of which waited for: 6 -> 0; matrix products, arithmetic and copies ran while one was open for 3% -> 0% of each run, Pallas kernels for 0% -> 0%
where the time goes in v1:
time: 24.7 us; the launch traced here: 24.3 us
  Pallas kernels  19.8 us (80%)
  local copies, waits for them, and re-layouts  2.99 us (12%)
  other arithmetic  1.45 us (6%)
    pallas_call x1, Pallas kernels, local(): pl.pallas_call(functools.partial(kernel, n_tm, n_rows), out_shape=jax.Sha...  19.8 us
    unnamed x1, local copies, waits for them, and re-layouts  1.62 us
    broadcast_in_dim x3, local copies, waits for them, and re-layouts, local(): jnp.broadcast_to(row.reshape(1, 2 * outputs), (8, 2 * outputs))  1.37 us
    concatenate x1, other arithmetic, local(): both_biases = jnp.concatenate([bias_upper, bias_upper])  0.83 us
    concatenate x1, other arithmetic, local(): jnp.concatenate([jnp.broadcast_to(row.reshape(1, 2 * outputs), (8, 2 * ou...  0.62 us

profile of v1, /device:TPU:0, one launch (start us, length us, event | category | flops | bytes accessed | tf_op | source)
XLA Modules:
  0.0 24.3 jit_solution(7192830391024251513)
XLA Ops:
  0.0 0.8 %pad_maximum_fusion.1 = f32[384]{0:T(512)S(1)} fusion(f32[192]{0:T(256)} %param.11), kind=kLoop, calls=%fused_computation.1 | loop fusion | flops 384 | bytes 2304 | tf_op jit(solution)/shard_map/concatenate | solution.py:324
  0.8 0.7 %broadcast_in_dim.6 = f32[8,384]{1,0:T(8,128)S(1)} broadcast(f32[384]{0:T(512)} %param.7), dimensions={1} | broadcast | bytes 13824 | tf_op jit(solution)/shard_map/broadcast_in_dim | solution.py:327
  1.5 0.7 %broadcast_in_dim.7 = f32[8,384]{1,0:T(8,128)S(1)} broadcast(f32[384]{0:T(512)} %param.9), dimensions={1} | broadcast | bytes 13824 | tf_op jit(solution)/shard_map/broadcast_in_dim | solution.py:327
  2.2 0.6 %pad_maximum_fusion.small_ref = f32[24,384]{1,0:T(8,128)} fusion(f32[8,384]{1,0:T(8,128)S(1)} %broadcast_in_dim.8, f32[8,384]{1,0:T(8,128)S(1)} %broadcast_in_dim.7, f32[8,384]{1,0:T(8,128)S(1)} %broadcast_in_dim.6), kind=kLoop, calls=%fused_computation | loop fusion | flops 18432 | bytes 73728 | tf_op jit(solution)/shard_map/concatenate | solution.py:325
  2.8 19.8 %shard_map.64 = bf16[16,6144]{1,0:T(8,128)(2,1)} custom-call(bf16[2,4,16,384]{3,2,1,0:T(8,128)(2,1)} %latent_ref.1, f32[24,384]{1,0:T(8,128)} %pad_maximum_fusion.small_ref, bf16[27,96,384]{2,1,0:T(8,128)(2,1)} %w1_hbm.1, bf16[9,192,384]{2,1,0:T(8,128)(2,1)} %bitcast.3), custom_call_target="tpu_custom_call" | custom-call | flops 1698693120 | bytes 4194304 | tf_op jit(solution)/shard_map/pallas_call | solution.py:331
  22.6 1.6 %copy.8 = bf16[2,8,6144]{2,1,0:T(8,128)(2,1)} copy(bf16[2,8,6144]{2,1,0:T(8,128)(2,1)} %bitcast.2) | data formatting | bytes 393216
  (1 shorter events, 0.0 us)

commit v2 on v1

--- a/solution.py
+++ b/solution.py
@@ -17,7 +17,9 @@
     n_tm,
     n_rows,
     latent_ref,
-    small_ref,
+    gain_ref,
+    bias1_ref,
+    bias2_ref,
     w1_hbm,
     wu_hbm,
     out_ref,
@@ -74,7 +76,7 @@
 
     values = latent_ref[...].astype(F32).reshape(cells, chans)
     mean_square = jnp.mean(values * values, axis=-1, keepdims=True)
-    scaled = values * lax.rsqrt(mean_square + 1e-06) * small_ref[pl.ds(0, 1)]
+    scaled = values * lax.rsqrt(mean_square + 1e-06) * gain_ref[...].reshape(1, chans)
     act = scaled / (1.0 + jnp.exp(-scaled))
     blank = jnp.zeros((cells, LANES - piece), F32)
     for s in range(n_tm):
@@ -225,7 +227,7 @@
             part_send[mate] = own[1 - lax.rem(me, 2)].astype(BF16)
             part_copy(mate).start()
 
-    summed = own[lax.rem(me, 2)] + small_ref[pl.ds(8, 1)]
+    summed = own[lax.rem(me, 2)] + bias1_ref[...].reshape(1, chans)
     summed = summed + latent_ref[...].astype(F32).reshape(cells, chans)
     for d in range(1, n_tm):
         s = lax.rem(me + n_tm - d, n_tm)
@@ -285,10 +287,10 @@
     nothing = jnp.zeros((1, frames * big, outputs), F32)
     before = jnp.concatenate([nothing, cols[0][: width - 1]], axis=0)
     after = jnp.concatenate([cols[2][1:], nothing], axis=0)
-    bias2 = small_ref[pl.ds(16, 1)].reshape(1, 1, 2 * outputs)
-    even = before + cols[1] + cols[2]
-    odd = cols[0] + cols[1] + after
-    both = (jnp.concatenate([even, odd], axis=-1) + bias2).astype(BF16)
+    bias2 = bias2_ref[...].reshape(1, 1, outputs)
+    even = before + cols[1] + cols[2] + bias2
+    odd = cols[0] + cols[1] + after + bias2
+    both = jnp.concatenate([even, odd], axis=-1).astype(BF16)
     for c in range(width):
         out_ref[:, pl.ds(c * 2 * outputs, 2 * outputs)] = both[c]
 
@@ -318,20 +320,13 @@
     all_frames = n_tm * frames
     depth = rows + 4
     vmem = pl.BlockSpec(memory_space=pltpu.VMEM)
-    hbm = pl.BlockSpec(memory_space=pl.ANY)
+    hbm = pl.BlockSpec(memory_space=pltpu.HBM)
     dma = pltpu.SemaphoreType.DMA
     flops = 2 * taps * piece * chans * all_frames * rows * width + 18 * 4 * cells * chans * outputs
-    both_biases = jnp.concatenate([bias_upper, bias_upper])
-    small = jnp.concatenate(
-        [
-            jnp.broadcast_to(row.reshape(1, 2 * outputs), (8, 2 * outputs))
-            for row in (gain_first, bias_first, both_biases)
-        ]
-    )
     decoded = pl.pallas_call(
         functools.partial(kernel, n_tm, n_rows),
         out_shape=jax.ShapeDtypeStruct((frames * 2 * rows, 2 * width * outputs), BF16),
-        in_specs=[vmem, vmem, hbm, hbm],
+        in_specs=[vmem, vmem, vmem, vmem, hbm, hbm],
         out_specs=vmem,
         scratch_shapes=[
             pltpu.VMEM(conv_first.shape, BF16),
@@ -361,7 +356,9 @@
         ),
     )(
         latent,
-        small,
+        gain_first,
+        bias_first,
+        bias_upper,
         conv_first,
         jnp.swapaxes(conv_upper, 1, 2),
     )

time: 24.7 us -> 21.8 us (0.88)
  other arithmetic: 1.45 us -> 0 us
  local copies, waits for them, and re-layouts: 2.99 us -> 1.62 us
    concatenate x2 -> x0, other arithmetic: 1.45 us -> none  [the longest x1 0.83 us: local(): both_biases = jnp.concatenate([bias_upper, bias_upper])]
    broadcast_in_dim x3 -> x0, local copies, waits for them, and re-layouts: 1.37 us -> none  [local(): jnp.broadcast_to(row.reshape(1, 2 * outputs), (8, 2 * outputs))]
where the time goes in v2:
time: 21.8 us; the launch traced here: 21.5 us
  Pallas kernels  19.8 us (91%)
  local copies, waits for them, and re-layouts  1.62 us (7%)
    pallas_call x1, Pallas kernels, local(): pl.pallas_call(functools.partial(kernel, n_tm, n_rows), out_shape=jax.Sha...  19.8 us
    unnamed x1, local copies, waits for them, and re-layouts  1.62 us

profile of v2, /device:TPU:0, one launch (start us, length us, event | category | flops | bytes accessed | tf_op | source)
XLA Modules:
  0.0 21.5 jit_solution(11488874414038390809)
XLA Ops:
  0.0 19.8 %shard_map.64 = bf16[16,6144]{1,0:T(8,128)(2,1)} custom-call(bf16[2,4,16,384]{3,2,1,0:T(8,128)(2,1)} %latent_ref.1, f32[384]{0:T(512)} %gain_ref.1, f32[384]{0:T(512)} %bias1_ref.1, f32[192]{0:T(256)} %bias2_ref.1, bf16[27,96,384]{2,1,0:T(8,128)(2,1)} %w1_hbm.1, bf16[9,192,384]{2,1,0:T(8,128)(2,1)} %bitcast.3), custom_call_target="tpu_custom_call" | custom-call | flops 1698693120 | bytes 4194304 | tf_op jit(solution)/shard_map/pallas_call | solution.py:326
  19.9 1.6 %copy.8 = bf16[2,8,6144]{2,1,0:T(8,128)(2,1)} copy(bf16[2,8,6144]{2,1,0:T(8,128)(2,1)} %bitcast.2) | data formatting | bytes 393216

commit v3 on v2

--- a/solution.py
+++ b/solution.py
@@ -192,15 +192,32 @@
 
     pairs = n_tm // 2
 
-    def part_copy(s):
-        return pltpu.make_async_remote_copy(
-            src_ref=part_send.at[s],
-            dst_ref=part_recv.at[me],
-            send_sem=part_send_sem.at[s],
-            recv_sem=part_recv_sem.at[me],
+    order = [0, rows - 1] + list(range(1, rows - 1))
+    spans = (pl.ds(0, 2), pl.ds(2, rows - 2))
+
+    def part_copy(s, kind):
+        return pltpu.make_async_remote_copy(
+            src_ref=part_send.at[s, :, spans[kind]],
+            dst_ref=part_recv.at[me, :, spans[kind]],
+            send_sem=part_send_sem.at[2 * s + kind],
+            recv_sem=part_recv_sem.at[2 * me + kind],
             device_id=(s, band),
             device_id_type=MESH,
         )
+
+    def part_arrival(s, kind):
+        return pltpu.make_async_remote_copy(
+            src_ref=part_send.at[s, :, spans[kind]],
+            dst_ref=part_recv.at[s, :, spans[kind]],
+            send_sem=part_send_sem.at[2 * s + kind],
+            recv_sem=part_recv_sem.at[2 * s + kind],
+            device_id=(s, band),
+            device_id_type=MESH,
+        )
+
+    def stage(s, sums):
+        for slot, row in enumerate(order):
+            part_send[s, :, slot] = sums[:, row].astype(BF16)
 
     for k in range(1, pairs + 1):
         pair = lax.rem(lax.div(me, 2) + k, pairs)
@@ -217,30 +234,34 @@
                 wpad[pl.ds(dt * 9 * LANES, 9 * LANES)],
                 preferred_element_type=F32,
             )
+        sums = total.reshape(2, frames, rows, width, chans)
         if k < pairs:
             for c in range(2):
-                part_send[2 * pair + c] = total[c * cells : (c + 1) * cells].astype(BF16)
-                part_copy(2 * pair + c).start()
+                stage(2 * pair + c, sums[c])
+            for kind in range(2):
+                for c in range(2):
+                    part_copy(2 * pair + c, kind).start()
         else:
-            own[...] = total.reshape(2, cells, chans)
+            own[...] = sums
             mate = 2 * lax.div(me, 2) + (1 - lax.rem(me, 2))
-            part_send[mate] = own[1 - lax.rem(me, 2)].astype(BF16)
-            part_copy(mate).start()
-
-    summed = own[lax.rem(me, 2)] + bias1_ref[...].reshape(1, chans)
-    summed = summed + latent_ref[...].astype(F32).reshape(cells, chans)
-    for d in range(1, n_tm):
-        s = lax.rem(me + n_tm - d, n_tm)
-        pltpu.make_async_remote_copy(
-            src_ref=part_send.at[s],
-            dst_ref=part_recv.at[s],
-            send_sem=part_send_sem.at[s],
-            recv_sem=part_recv_sem.at[s],
-            device_id=(s, band),
-            device_id_type=MESH,
-        ).wait_recv()
-        summed = summed + part_recv[s].astype(F32)
-    block[:, pl.ds(1, rows)] = summed.astype(BF16).reshape(frames, rows, width, chans)
+            stage(mate, own[1 - lax.rem(me, 2)])
+            for kind in range(2):
+                part_copy(mate, kind).start()
+
+    bias1 = bias1_ref[...].reshape(1, 1, chans)
+
+    def finish(kind):
+        for d in range(1, n_tm):
+            part_arrival(lax.rem(me + n_tm - d, n_tm), kind).wait_recv()
+        for slot, row in enumerate(order):
+            if (slot >= 2) != (kind == 1):
+                continue
+            summed = own[lax.rem(me, 2), :, row] + bias1 + latent_ref[:, row].astype(F32)
+            for d in range(1, n_tm):
+                summed = summed + part_recv[lax.rem(me + n_tm - d, n_tm), :, slot].astype(F32)
+            block[:, row + 1] = summed.astype(BF16)
+
+    finish(0)
 
     def row_copy(kind, row, where, to):
         return pltpu.make_async_remote_copy(
@@ -260,6 +281,7 @@
     def _():
         row_copy(1, 1, rows + 1, above).start()
 
+    finish(1)
     load_wu.wait()
 
     @pl.when(has_above)
@@ -297,7 +319,8 @@
     for d in range(1, n_tm):
         s = lax.rem(me + d, n_tm)
         main_copy(s).wait_send()
-        part_copy(s).wait_send()
+        for kind in range(2):
+            part_copy(s, kind).wait_send()
 
     @pl.when(has_below)
     def _():
@@ -335,16 +358,16 @@
             pltpu.VMEM((n_tm, frames, rows, width, LANES), BF16),
             pltpu.VMEM((all_frames, rows + 2, width, LANES), BF16),
             pltpu.VMEM((3, all_frames + 2, rows + 2, width, LANES), BF16),
-            pltpu.VMEM((n_tm, cells, chans), BF16),
-            pltpu.VMEM((n_tm, cells, chans), BF16),
-            pltpu.VMEM((2, cells, chans), F32),
+            pltpu.VMEM((n_tm, frames, rows, width, chans), BF16),
+            pltpu.VMEM((n_tm, frames, rows, width, chans), BF16),
+            pltpu.VMEM((2, frames, rows, width, chans), F32),
             pltpu.VMEM((frames, depth, width, chans), BF16),
             pltpu.VMEM((6 * cells, frames * depth * width), BF16),
             dma((2,)),
             dma((3 * n_tm,)),
             dma((3 * n_tm,)),
-            dma((n_tm,)),
-            dma((n_tm,)),
+            dma((2 * n_tm,)),
+            dma((2 * n_tm,)),
             dma((2,)),
             dma((2,)),
         ],

time: 21.8 us -> 20.7 us (0.950)
  Pallas kernels: 19.8 us -> 18.9 us
    pallas_call x1, Pallas kernels: 19.8 us -> 18.9 us  [local(): pl.pallas_call(functools.partial(kernel, n_tm, n_rows), out_shape=jax.Sha...]
where the time goes in v3:
time: 20.7 us; the launch traced here: 20.5 us
  Pallas kernels  18.9 us (91%)
  local copies, waits for them, and re-layouts  1.62 us (8%)
    pallas_call x1, Pallas kernels, local(): pl.pallas_call(functools.partial(kernel, n_tm, n_rows), out_shape=jax.Sha...  18.9 us
    unnamed x1, local copies, waits for them, and re-layouts  1.62 us

profile of v3, /device:TPU:0, one launch (start us, length us, event | category | flops | bytes accessed | tf_op | source)
XLA Modules:
  0.0 20.5 jit_solution(16800300782026572765)
XLA Ops:
  0.0 18.9 %shard_map.64 = bf16[16,6144]{1,0:T(8,128)(2,1)} custom-call(bf16[2,4,16,384]{3,2,1,0:T(8,128)(2,1)} %latent_ref.1, f32[384]{0:T(512)} %gain_ref.1, f32[384]{0:T(512)} %bias1_ref.1, f32[192]{0:T(256)} %bias2_ref.1, bf16[27,96,384]{2,1,0:T(8,128)(2,1)} %w1_hbm.1, bf16[9,192,384]{2,1,0:T(8,128)(2,1)} %bitcast.3), custom_call_target="tpu_custom_call" | custom-call | flops 1698693120 | bytes 4194304 | tf_op jit(solution)/shard_map/pallas_call | solution.py:349
  18.9 1.6 %copy.8 = bf16[2,8,6144]{2,1,0:T(8,128)(2,1)} copy(bf16[2,8,6144]{2,1,0:T(8,128)(2,1)} %bitcast.2) | data formatting | bytes 393216

commit v4 on v3

--- a/solution.py
+++ b/solution.py
@@ -372,7 +372,7 @@
             dma((2,)),
         ],
         compiler_params=pltpu.CompilerParams(
-            collective_id=0, has_side_effects=True, vmem_limit_bytes=60 * 1024 * 1024
+            collective_id=0, has_side_effects=True, vmem_limit_bytes=53 * 1024 * 1024
         ),
         cost_estimate=pl.CostEstimate(
             flops=flops, bytes_accessed=4 * 1024 * 1024, transcendentals=cells * chans

time: 20.7 us -> 21.2 us (1.024)
  local copies, waits for them, and re-layouts: 1.62 us -> 3.61 us
  Pallas kernels: 18.9 us -> 17.3 us
    unnamed x1 -> x9, local copies, waits for them, and re-layouts: 1.62 us -> 3.61 us
    pallas_call x1, Pallas kernels: 18.9 us -> 17.3 us  [local(): pl.pallas_call(functools.partial(kernel, n_tm, n_rows), out_shape=jax.Sha...]
where the time goes in v4:
time: 21.2 us; the launch traced here: 21 us
  Pallas kernels  17.3 us (82%)
  local copies, waits for them, and re-layouts  3.61 us (17%)
    pallas_call x1, Pallas kernels, local(): pl.pallas_call(functools.partial(kernel, n_tm, n_rows), out_shape=jax.Sha...  17.3 us
    unnamed x9, local copies, waits for them, and re-layouts  3.61 us

profile of v4, /device:TPU:0, one launch (start us, length us, event | category | flops | bytes accessed | tf_op | source)
XLA Modules:
  0.0 21.0 jit_solution(5671289657348489863)
XLA Ops:
  0.0 0.0 copy-start
  0.0 0.9 %copy-done = bf16[2,4,16,384]{3,2,1,0:T(8,128)(2,1)S(1)} copy-done((bf16[2,4,16,384]{3,2,1,0:T(8,128)(2,1)S(1)}, bf16[2,4,16,384]{3,2,1,0:T(8,128)(2,1)}, u32[]{:S(2)}) %copy-start) | copy-done | bytes 98328
  0.9 0.0 copy-start.1
  0.9 0.7 %copy-done.1 = f32[384]{0:T(512)S(1)} copy-done((f32[384]{0:T(512)S(1)}, f32[384]{0:T(512)}, u32[]{:S(2)}) %copy-start.1) | copy-done | bytes 1560
  1.6 0.0 copy-start.2
  1.6 0.7 %copy-done.2 = f32[384]{0:T(512)S(1)} copy-done((f32[384]{0:T(512)S(1)}, f32[384]{0:T(512)}, u32[]{:S(2)}) %copy-start.2) | copy-done | bytes 1560
  2.3 0.0 copy-start.3
  2.3 0.7 %copy-done.3 = f32[192]{0:T(256)S(1)} copy-done((f32[192]{0:T(256)S(1)}, f32[192]{0:T(256)}, u32[]{:S(2)}) %copy-start.3) | copy-done | bytes 792
  2.9 17.3 %shard_map.64 = bf16[16,6144]{1,0:T(8,128)(2,1)S(1)} custom-call(bf16[2,4,16,384]{3,2,1,0:T(8,128)(2,1)S(1)} %copy-done, f32[384]{0:T(512)S(1)} %copy-done.1, f32[384]{0:T(512)S(1)} %copy-done.2, f32[192]{0:T(256)S(1)} %copy-done.3, bf16[27,96,384]{2,1,0:T(8,128)(2,1)} %w1_hbm.1, bf16[9,192,384]{2,1,0:T(8,128)(2,1)} %bitcast.3), custom_call_target="tpu_custom_call" | custom-call | flops 1698693120 | bytes 4194304 | tf_op jit(solution)/shard_map/pallas_call | solution.py:349
  20.3 0.7 %copy.8 = bf16[2,8,6144]{2,1,0:T(8,128)(2,1)} copy(bf16[2,8,6144]{2,1,0:T(8,128)(2,1)S(1)} %bitcast.2) | data formatting | bytes 393216
Async XLA Ops:
  0.0 0.9 %copy-start = (bf16[2,4,16,384]{3,2,1,0:T(8,128)(2,1)S(1)}, bf16[2,4,16,384]{3,2,1,0:T(8,128)(2,1)}, u32[]{:S(2)}) copy-start(bf16[2,4,16,384]{3,2,1,0:T(8,128)(2,1)} %latent_ref.1) | copy-start | bytes 294916
  0.9 0.7 %copy-start.1 = (f32[384]{0:T(512)S(1)}, f32[384]{0:T(512)}, u32[]{:S(2)}) copy-start(f32[384]{0:T(512)} %gain_ref.1) | copy-start | bytes 4612
  1.6 0.7 %copy-start.2 = (f32[384]{0:T(512)S(1)}, f32[384]{0:T(512)}, u32[]{:S(2)}) copy-start(f32[384]{0:T(512)} %bias1_ref.1) | copy-start | bytes 4612
  2.3 0.7 %copy-start.3 = (f32[192]{0:T(256)S(1)}, f32[192]{0:T(256)}, u32[]{:S(2)}) copy-start(f32[192]{0:T(256)} %bias2_ref.1) | copy-start | bytes 2308

commit v5 on v3

--- a/solution.py
+++ b/solution.py
@@ -16,13 +16,17 @@
 def kernel(
     n_tm,
     n_rows,
+    latent_hbm,
+    gain_hbm,
+    bias1_hbm,
+    bias2_hbm,
+    w1_hbm,
+    wu_hbm,
+    out_ref,
     latent_ref,
     gain_ref,
     bias1_ref,
     bias2_ref,
-    w1_hbm,
-    wu_hbm,
-    out_ref,
     w1_ref,
     wpad,
     wu_ref,
@@ -53,10 +57,14 @@
     has_above = band > 0
     has_below = band < n_rows - 1
 
-    load_w1 = pltpu.make_async_copy(w1_hbm, w1_ref, load_sem.at[0])
-    load_w1.start()
-    load_wu = pltpu.make_async_copy(wu_hbm, wu_ref, load_sem.at[1])
-    load_wu.start()
+    load_latent = pltpu.make_async_copy(latent_hbm, latent_ref, load_sem.at[0])
+    load_gain = pltpu.make_async_copy(gain_hbm, gain_ref, load_sem.at[1])
+    load_w1 = pltpu.make_async_copy(w1_hbm, w1_ref, load_sem.at[2])
+    load_bias1 = pltpu.make_async_copy(bias1_hbm, bias1_ref, load_sem.at[3])
+    load_wu = pltpu.make_async_copy(wu_hbm, wu_ref, load_sem.at[4])
+    load_bias2 = pltpu.make_async_copy(bias2_hbm, bias2_ref, load_sem.at[5])
+    for load in (load_latent, load_gain, load_w1, load_bias1, load_wu, load_bias2):
+        load.start()
 
     barrier = pltpu.get_barrier_semaphore()
     for d in range(1, n_tm):
@@ -74,6 +82,8 @@
         for s in range(n_tm):
             pl.semaphore_signal(barrier, inc=1, device_id=(s, below), device_id_type=MESH)
 
+    load_latent.wait()
+    load_gain.wait()
     values = latent_ref[...].astype(F32).reshape(cells, chans)
     mean_square = jnp.mean(values * values, axis=-1, keepdims=True)
     scaled = values * lax.rsqrt(mean_square + 1e-06) * gain_ref[...].reshape(1, chans)
@@ -248,6 +258,7 @@
             for kind in range(2):
                 part_copy(mate, kind).start()
 
+    load_bias1.wait()
     bias1 = bias1_ref[...].reshape(1, 1, chans)
 
     def finish(kind):
@@ -283,6 +294,7 @@
 
     finish(1)
     load_wu.wait()
+    load_bias2.wait()
 
     @pl.when(has_above)
     def _():
@@ -343,15 +355,19 @@
     all_frames = n_tm * frames
     depth = rows + 4
     vmem = pl.BlockSpec(memory_space=pltpu.VMEM)
-    hbm = pl.BlockSpec(memory_space=pltpu.HBM)
+    hbm = pl.BlockSpec(memory_space=pl.ANY)
     dma = pltpu.SemaphoreType.DMA
     flops = 2 * taps * piece * chans * all_frames * rows * width + 18 * 4 * cells * chans * outputs
     decoded = pl.pallas_call(
         functools.partial(kernel, n_tm, n_rows),
         out_shape=jax.ShapeDtypeStruct((frames * 2 * rows, 2 * width * outputs), BF16),
-        in_specs=[vmem, vmem, vmem, vmem, hbm, hbm],
+        in_specs=[hbm] * 6,
         out_specs=vmem,
         scratch_shapes=[
+            pltpu.VMEM(latent.shape, BF16),
+            pltpu.VMEM((chans,), F32),
+            pltpu.VMEM((chans,), F32),
+            pltpu.VMEM((outputs,), F32),
             pltpu.VMEM(conv_first.shape, BF16),
             pltpu.VMEM((taps * LANES, chans), BF16),
             pltpu.VMEM((9, outputs, chans), BF16),
@@ -363,7 +379,7 @@
             pltpu.VMEM((2, frames, rows, width, chans), F32),
             pltpu.VMEM((frames, depth, width, chans), BF16),
             pltpu.VMEM((6 * cells, frames * depth * width), BF16),
-            dma((2,)),
+            dma((6,)),
             dma((3 * n_tm,)),
             dma((3 * n_tm,)),
             dma((2 * n_tm,)),

time: 20.7 us -> 19.8 us (0.957)
  Pallas kernels: 18.9 us -> 18 us
    pallas_call x1, Pallas kernels: 18.9 us -> 18 us  [local(): pl.pallas_call(functools.partial(kernel, n_tm, n_rows), out_shape=jax.Sha...]
where the time goes in v5:
time: 19.8 us; the launch traced here: 19.7 us
  Pallas kernels  18 us (91%)
  local copies, waits for them, and re-layouts  1.62 us (8%)
    pallas_call x1, Pallas kernels, local(): pl.pallas_call(functools.partial(kernel, n_tm, n_rows), out_shape=jax.Sha...  18 us
    unnamed x1, local copies, waits for them, and re-layouts  1.62 us

profile of v5, /device:TPU:0, one launch (start us, length us, event | category | flops | bytes accessed | tf_op | source)
XLA Modules:
  0.0 19.7 jit_solution(16076194255132577449)
XLA Ops:
  0.0 18.0 %shard_map.64 = bf16[16,6144]{1,0:T(8,128)(2,1)} custom-call(bf16[2,4,16,384]{3,2,1,0:T(8,128)(2,1)} %latent_hbm.1, f32[384]{0:T(512)} %gain_hbm.1, f32[384]{0:T(512)} %bias1_hbm.1, f32[192]{0:T(256)} %bias2_hbm.1, bf16[27,96,384]{2,1,0:T(8,128)(2,1)} %w1_hbm.1, bf16[9,192,384]{2,1,0:T(8,128)(2,1)} %bitcast.3), custom_call_target="tpu_custom_call" | custom-call | flops 1698693120 | bytes 4194304 | tf_op jit(solution)/shard_map/pallas_call | solution.py:361
  18.0 1.6 %copy.8 = bf16[2,8,6144]{2,1,0:T(8,128)(2,1)} copy(bf16[2,8,6144]{2,1,0:T(8,128)(2,1)} %bitcast.2) | data formatting | bytes 393216

commit v6 on v5

--- a/solution.py
+++ b/solution.py
@@ -11,6 +11,16 @@
 F32 = jnp.float32
 BF16 = jnp.bfloat16
 LANES = 128
+
+
+def quotient(number, by):
+    if by & (by - 1):
+        return number // by
+    return lax.shift_right_logical(number, by.bit_length() - 1)
+
+
+def remainder(number, by):
+    return number % by if by & (by - 1) else number & (by - 1)
 
 
 def kernel(
@@ -152,15 +162,6 @@
     block[:, pl.ds(rows + 2, depth - rows - 2)] = jnp.zeros(
         (frames, depth - rows - 2, width, chans), BF16
     )
-    at = lax.broadcasted_iota(jnp.int32, (pick.shape[0], 1), 0)
-    to = lax.broadcasted_iota(jnp.int32, pick.shape, 1)
-    row_tap = at // (frames * width * big)
-    col = (at // (frames * big)) % width
-    frame = (at // big) % frames
-    line = at % big
-    source = frame * (depth * width) + ((line + row_tap + 1) // 2) * width + col
-    pick[...] = jnp.where(to == source, 1.0, 0.0).astype(BF16)
-
     load_w1.wait()
     spare = jnp.zeros((LANES - piece, chans), BF16)
     for tap in range(taps):
@@ -192,7 +193,7 @@
 
     tall = all_frames * (rows + 2) * width
     flat = recv[...].astype(F32).reshape(tall, LANES)
-    column = lax.broadcasted_iota(jnp.int32, (tall, LANES), 0) % width
+    column = remainder(lax.broadcasted_iota(jnp.int32, (tall, LANES), 0), width)
     left = jnp.where(column == 0, 0.0, pltpu.roll(flat, 1, 0))
     right = jnp.where(column == width - 1, 0.0, pltpu.roll(flat, tall - 1, 0))
     shape = (all_frames, rows + 2, width, LANES)
@@ -257,6 +258,15 @@
             stage(mate, own[1 - lax.rem(me, 2)])
             for kind in range(2):
                 part_copy(mate, kind).start()
+
+    at = lax.broadcasted_iota(jnp.int32, (pick.shape[0], 1), 0)
+    to = lax.broadcasted_iota(jnp.int32, pick.shape, 1)
+    row_tap = quotient(at, frames * width * big)
+    col = remainder(quotient(at, frames * big), width)
+    frame = remainder(quotient(at, big), frames)
+    line = remainder(at, big)
+    source = frame * (depth * width) + quotient(line + row_tap + 1, 2) * width + col
+    pick[...] = jnp.where(to == source, 1.0, 0.0).astype(BF16)
 
     load_bias1.wait()
     bias1 = bias1_ref[...].reshape(1, 1, chans)

time: 19.8 us -> 20 us (1.010)
    pallas_call x1, Pallas kernels: 18 us -> 18.2 us  [local(): pl.pallas_call(functools.partial(kernel, n_tm, n_rows), out_shape=jax.Sha...]
where the time goes in v6:
time: 20 us; the launch traced here: 19.9 us
  Pallas kernels  18.2 us (91%)
  local copies, waits for them, and re-layouts  1.62 us (8%)
    pallas_call x1, Pallas kernels, local(): pl.pallas_call(functools.partial(kernel, n_tm, n_rows), out_shape=jax.Sha...  18.2 us
    unnamed x1, local copies, waits for them, and re-layouts  1.62 us

profile of v6, /device:TPU:0, one launch (start us, length us, event | category | flops | bytes accessed | tf_op | source)
XLA Modules:
  0.0 19.9 jit_solution(11930363438339614820)
XLA Ops:
  0.0 18.2 %shard_map.64 = bf16[16,6144]{1,0:T(8,128)(2,1)} custom-call(bf16[2,4,16,384]{3,2,1,0:T(8,128)(2,1)} %latent_hbm.1, f32[384]{0:T(512)} %gain_hbm.1, f32[384]{0:T(512)} %bias1_hbm.1, f32[192]{0:T(256)} %bias2_hbm.1, bf16[27,96,384]{2,1,0:T(8,128)(2,1)} %w1_hbm.1, bf16[9,192,384]{2,1,0:T(8,128)(2,1)} %bitcast.3), custom_call_target="tpu_custom_call" | custom-call | flops 1698693120 | bytes 4194304 | tf_op jit(solution)/shard_map/pallas_call | solution.py:371
  18.3 1.6 %copy.8 = bf16[2,8,6144]{2,1,0:T(8,128)(2,1)} copy(bf16[2,8,6144]{2,1,0:T(8,128)(2,1)} %bitcast.2) | data formatting | bytes 393216

commit v7 on v6

--- a/solution.py
+++ b/solution.py
@@ -45,6 +45,9 @@
     shifted,
     part_send,
     part_recv,
+    relay_send,
+    relay_recv,
+    held,
     own,
     block,
     pick,
@@ -53,6 +56,8 @@
     act_recv_sem,
     part_send_sem,
     part_recv_sem,
+    relay_send_sem,
+    relay_recv_sem,
     row_send_sem,
     row_recv_sem,
 ):
@@ -162,6 +167,15 @@
     block[:, pl.ds(rows + 2, depth - rows - 2)] = jnp.zeros(
         (frames, depth - rows - 2, width, chans), BF16
     )
+    at = lax.broadcasted_iota(jnp.int32, (pick.shape[0], 1), 0)
+    to = lax.broadcasted_iota(jnp.int32, pick.shape, 1)
+    row_tap = quotient(at, frames * width * big)
+    col = remainder(quotient(at, frames * big), width)
+    frame = remainder(quotient(at, big), frames)
+    line = remainder(at, big)
+    source = frame * (depth * width) + quotient(line + row_tap + 1, 2) * width + col
+    pick[...] = jnp.where(to == source, 1.0, 0.0).astype(BF16)
+
     load_w1.wait()
     spare = jnp.zeros((LANES - piece, chans), BF16)
     for tap in range(taps):
@@ -230,56 +244,62 @@
         for slot, row in enumerate(order):
             part_send[s, :, slot] = sums[:, row].astype(BF16)
 
-    for k in range(1, pairs + 1):
-        pair = lax.rem(lax.div(me, 2) + k, pairs)
-        total = jnp.zeros((2 * cells, chans), F32)
+    core = lax.rem(me, 2)
+    mate = 2 * lax.div(me, 2) + (1 - core)
+    elsewhere = [2 * lax.rem(lax.div(me, 2) + k, pairs) for k in range(1, pairs)]
+
+    def partial(start, count):
+        total = jnp.zeros((count * cells, chans), F32)
         for dt in range(3):
             windows = []
             for dy in range(3):
                 for dx in range(3):
-                    start = pair * (2 * frames) + dt
-                    view = shifted[dx, pl.ds(start, 2 * frames), pl.ds(dy, rows)]
-                    windows.append(view.reshape(2 * cells, LANES))
+                    view = shifted[dx, pl.ds(start * frames + dt, count * frames), pl.ds(dy, rows)]
+                    windows.append(view.reshape(count * cells, LANES))
             total = total + jnp.dot(
                 jnp.concatenate(windows, axis=1),
                 wpad[pl.ds(dt * 9 * LANES, 9 * LANES)],
                 preferred_element_type=F32,
             )
-        sums = total.reshape(2, frames, rows, width, chans)
-        if k < pairs:
-            for c in range(2):
-                stage(2 * pair + c, sums[c])
-            for kind in range(2):
-                for c in range(2):
-                    part_copy(2 * pair + c, kind).start()
-        else:
-            own[...] = sums
-            mate = 2 * lax.div(me, 2) + (1 - lax.rem(me, 2))
-            stage(mate, own[1 - lax.rem(me, 2)])
-            for kind in range(2):
-                part_copy(mate, kind).start()
-
-    at = lax.broadcasted_iota(jnp.int32, (pick.shape[0], 1), 0)
-    to = lax.broadcasted_iota(jnp.int32, pick.shape, 1)
-    row_tap = quotient(at, frames * width * big)
-    col = remainder(quotient(at, frames * big), width)
-    frame = remainder(quotient(at, big), frames)
-    line = remainder(at, big)
-    source = frame * (depth * width) + quotient(line + row_tap + 1, 2) * width + col
-    pick[...] = jnp.where(to == source, 1.0, 0.0).astype(BF16)
-
+        return total.reshape(count, frames, rows, width, chans)
+
+    def relay(k):
+        return pltpu.make_async_remote_copy(
+            src_ref=relay_send.at[k],
+            dst_ref=relay_recv.at[k],
+            send_sem=relay_send_sem.at[k],
+            recv_sem=relay_recv_sem.at[k],
+            device_id=(mate, band),
+            device_id_type=MESH,
+        )
+
+    for k, first in enumerate(elsewhere):
+        relay_send[k] = partial(first + (1 - core), 1)[0].astype(BF16)
+        relay(k).start()
+        held[k] = partial(first + core, 1)[0]
+    for k, first in enumerate(elsewhere):
+        relay(k).wait_recv()
+        stage(first + core, held[k] + relay_recv[k].astype(F32))
+        for kind in range(2):
+            part_copy(first + core, kind).start()
+    own[...] = partial(2 * lax.div(me, 2), 2)
+    stage(mate, own[1 - core])
+    for kind in range(2):
+        part_copy(mate, kind).start()
+
+    sources = [mate] + [first + core for first in elsewhere]
     load_bias1.wait()
     bias1 = bias1_ref[...].reshape(1, 1, chans)
 
     def finish(kind):
-        for d in range(1, n_tm):
-            part_arrival(lax.rem(me + n_tm - d, n_tm), kind).wait_recv()
+        for s in sources:
+            part_arrival(s, kind).wait_recv()
         for slot, row in enumerate(order):
             if (slot >= 2) != (kind == 1):
                 continue
-            summed = own[lax.rem(me, 2), :, row] + bias1 + latent_ref[:, row].astype(F32)
-            for d in range(1, n_tm):
-                summed = summed + part_recv[lax.rem(me + n_tm - d, n_tm), :, slot].astype(F32)
+            summed = own[core, :, row] + bias1 + latent_ref[:, row].astype(F32)
+            for s in sources:
+                summed = summed + part_recv[s, :, slot].astype(F32)
             block[:, row + 1] = summed.astype(BF16)
 
     finish(0)
@@ -341,8 +361,11 @@
     for d in range(1, n_tm):
         s = lax.rem(me + d, n_tm)
         main_copy(s).wait_send()
+    for s in sources:
         for kind in range(2):
             part_copy(s, kind).wait_send()
+    for k in range(pairs - 1):
+        relay(k).wait_send()
 
     @pl.when(has_below)
     def _():
@@ -364,6 +387,7 @@
     cells = frames * rows * width
     all_frames = n_tm * frames
     depth = rows + 4
+    others = n_tm // 2 - 1
     vmem = pl.BlockSpec(memory_space=pltpu.VMEM)
     hbm = pl.BlockSpec(memory_space=pl.ANY)
     dma = pltpu.SemaphoreType.DMA
@@ -386,6 +410,9 @@
             pltpu.VMEM((3, all_frames + 2, rows + 2, width, LANES), BF16),
             pltpu.VMEM((n_tm, frames, rows, width, chans), BF16),
             pltpu.VMEM((n_tm, frames, rows, width, chans), BF16),
+            pltpu.VMEM((others, frames, rows, width, chans), BF16),
+            pltpu.VMEM((others, frames, rows, width, chans), BF16),
+            pltpu.VMEM((others, frames, rows, width, chans), F32),
             pltpu.VMEM((2, frames, rows, width, chans), F32),
             pltpu.VMEM((frames, depth, width, chans), BF16),
             pltpu.VMEM((6 * cells, frames * depth * width), BF16),
@@ -394,6 +421,8 @@
             dma((3 * n_tm,)),
             dma((2 * n_tm,)),
             dma((2 * n_tm,)),
+            dma((others,)),
+            dma((others,)),
             dma((2,)),
             dma((2,)),
         ],

time: 20 us -> 20.3 us (1.015)
  Pallas kernels: 18.2 us -> 18.6 us
    pallas_call x1, Pallas kernels: 18.2 us -> 18.6 us  [local(): pl.pallas_call(functools.partial(kernel, n_tm, n_rows), out_shape=jax.Sha...]
where the time goes in v7:
time: 20.3 us; the launch traced here: 20.2 us
  Pallas kernels  18.6 us (92%)
  local copies, waits for them, and re-layouts  1.62 us (8%)
    pallas_call x1, Pallas kernels, local(): pl.pallas_call(functools.partial(kernel, n_tm, n_rows), out_shape=jax.Sha...  18.6 us
    unnamed x1, local copies, waits for them, and re-layouts  1.62 us

profile of v7, /device:TPU:0, one launch (start us, length us, event | category | flops | bytes accessed | tf_op | source)
XLA Modules:
  0.0 20.2 jit_solution(8708934196676902945)
XLA Ops:
  0.0 18.6 %shard_map.64 = bf16[16,6144]{1,0:T(8,128)(2,1)} custom-call(bf16[2,4,16,384]{3,2,1,0:T(8,128)(2,1)} %latent_hbm.1, f32[384]{0:T(512)} %gain_hbm.1, f32[384]{0:T(512)} %bias1_hbm.1, f32[192]{0:T(256)} %bias2_hbm.1, bf16[27,96,384]{2,1,0:T(8,128)(2,1)} %w1_hbm.1, bf16[9,192,384]{2,1,0:T(8,128)(2,1)} %bitcast.3), custom_call_target="tpu_custom_call" | custom-call | flops 1698693120 | bytes 4194304 | tf_op jit(solution)/shard_map/pallas_call | solution.py:395
  18.6 1.6 %copy.8 = bf16[2,8,6144]{2,1,0:T(8,128)(2,1)} copy(bf16[2,8,6144]{2,1,0:T(8,128)(2,1)} %bitcast.2) | data formatting | bytes 393216

commit v8 on v6

--- a/solution.py
+++ b/solution.py
@@ -40,6 +40,7 @@
     w1_ref,
     wpad,
     wu_ref,
+    upper,
     send,
     recv,
     shifted,
@@ -162,6 +163,15 @@
     block[:, pl.ds(rows + 2, depth - rows - 2)] = jnp.zeros(
         (frames, depth - rows - 2, width, chans), BF16
     )
+    at = lax.broadcasted_iota(jnp.int32, (pick.shape[0], 1), 0)
+    to = lax.broadcasted_iota(jnp.int32, pick.shape, 1)
+    row_tap = quotient(at, frames * width * big)
+    col = remainder(quotient(at, frames * big), width)
+    frame = remainder(quotient(at, big), frames)
+    line = remainder(at, big)
+    source = frame * (depth * width) + quotient(line + row_tap + 1, 2) * width + col
+    pick[...] = jnp.where(to == source, 1.0, 0.0).astype(BF16)
+
     load_w1.wait()
     spare = jnp.zeros((LANES - piece, chans), BF16)
     for tap in range(taps):
@@ -259,14 +269,10 @@
             for kind in range(2):
                 part_copy(mate, kind).start()
 
-    at = lax.broadcasted_iota(jnp.int32, (pick.shape[0], 1), 0)
-    to = lax.broadcasted_iota(jnp.int32, pick.shape, 1)
-    row_tap = quotient(at, frames * width * big)
-    col = remainder(quotient(at, frames * big), width)
-    frame = remainder(quotient(at, big), frames)
-    line = remainder(at, big)
-    source = frame * (depth * width) + quotient(line + row_tap + 1, 2) * width + col
-    pick[...] = jnp.where(to == source, 1.0, 0.0).astype(BF16)
+    load_wu.wait()
+    for dx in range(3):
+        taken = jnp.concatenate([wu_ref[dx], wu_ref[3 + dx], wu_ref[6 + dx]], axis=1)
+        upper[dx] = taken.T
 
     load_bias1.wait()
     bias1 = bias1_ref[...].reshape(1, 1, chans)
@@ -303,7 +309,6 @@
         row_copy(1, 1, rows + 1, above).start()
 
     finish(1)
-    load_wu.wait()
     load_bias2.wait()
 
     @pl.when(has_above)
@@ -323,10 +328,7 @@
     lines = jnp.concatenate([spread[k * high : (k + 1) * high] for k in range(3)], axis=1)
     cols = []
     for dx in range(3):
-        weights = jnp.concatenate([wu_ref[dx], wu_ref[3 + dx], wu_ref[6 + dx]], axis=1)
-        product = lax.dot_general(
-            lines, weights, (((1,), (1,)), ((), ())), preferred_element_type=F32
-        )
+        product = jnp.dot(lines, upper[dx], preferred_element_type=F32)
         cols.append(product.reshape(width, frames * big, outputs))
     nothing = jnp.zeros((1, frames * big, outputs), F32)
     before = jnp.concatenate([nothing, cols[0][: width - 1]], axis=0)
@@ -381,6 +383,7 @@
             pltpu.VMEM(conv_first.shape, BF16),
             pltpu.VMEM((taps * LANES, chans), BF16),
             pltpu.VMEM((9, outputs, chans), BF16),
+            pltpu.VMEM((3, 3 * chans, outputs), BF16),
             pltpu.VMEM((n_tm, frames, rows, width, LANES), BF16),
             pltpu.VMEM((all_frames, rows + 2, width, LANES), BF16),
             pltpu.VMEM((3, all_frames + 2, rows + 2, width, LANES), BF16),

time: 20 us -> 19.8 us (0.990)
  no operation moved by 1% of the time
where the time goes in v8:
time: 19.8 us; the launch traced here: 19.7 us
  Pallas kernels  18.1 us (91%)
  local copies, waits for them, and re-layouts  1.62 us (8%)
    pallas_call x1, Pallas kernels, local(): pl.pallas_call(functools.partial(kernel, n_tm, n_rows), out_shape=jax.Sha...  18.1 us
    unnamed x1, local copies, waits for them, and re-layouts  1.62 us

profile of v8, /device:TPU:0, one launch (start us, length us, event | category | flops | bytes accessed | tf_op | source)
XLA Modules:
  0.0 19.7 jit_solution(11146604696453038712)
XLA Ops:
  0.0 18.1 %shard_map.64 = bf16[16,6144]{1,0:T(8,128)(2,1)} custom-call(bf16[2,4,16,384]{3,2,1,0:T(8,128)(2,1)} %latent_hbm.1, f32[384]{0:T(512)} %gain_hbm.1, f32[384]{0:T(512)} %bias1_hbm.1, f32[192]{0:T(256)} %bias2_hbm.1, bf16[27,96,384]{2,1,0:T(8,128)(2,1)} %w1_hbm.1, bf16[9,192,384]{2,1,0:T(8,128)(2,1)} %bitcast.3), custom_call_target="tpu_custom_call" | custom-call | flops 1698693120 | bytes 4194304 | tf_op jit(solution)/shard_map/pallas_call | solution.py:373
  18.1 1.6 %copy.8 = bf16[2,8,6144]{2,1,0:T(8,128)(2,1)} copy(bf16[2,8,6144]{2,1,0:T(8,128)(2,1)} %bitcast.2) | data formatting | bytes 393216

commit v9 on v5

--- a/solution.py
+++ b/solution.py
@@ -231,19 +231,16 @@
 
     for k in range(1, pairs + 1):
         pair = lax.rem(lax.div(me, 2) + k, pairs)
-        total = jnp.zeros((2 * cells, chans), F32)
+        windows = []
         for dt in range(3):
-            windows = []
             for dy in range(3):
                 for dx in range(3):
                     start = pair * (2 * frames) + dt
                     view = shifted[dx, pl.ds(start, 2 * frames), pl.ds(dy, rows)]
                     windows.append(view.reshape(2 * cells, LANES))
-            total = total + jnp.dot(
-                jnp.concatenate(windows, axis=1),
-                wpad[pl.ds(dt * 9 * LANES, 9 * LANES)],
-                preferred_element_type=F32,
-            )
+        total = jnp.dot(
+            jnp.concatenate(windows, axis=1), wpad[...], preferred_element_type=F32
+        )
         sums = total.reshape(2, frames, rows, width, chans)
         if k < pairs:
             for c in range(2):

time: 19.8 us -> 19.8 us (level)
  no operation moved by 1% of the time
where the time goes in v9:
time: 19.8 us; the launch traced here: 19.7 us
  Pallas kernels  18.1 us (91%)
  local copies, waits for them, and re-layouts  1.62 us (8%)
    pallas_call x1, Pallas kernels, local(): pl.pallas_call(functools.partial(kernel, n_tm, n_rows), out_shape=jax.Sha...  18.1 us
    unnamed x1, local copies, waits for them, and re-layouts  1.62 us

profile of v9, /device:TPU:0, one launch (start us, length us, event | category | flops | bytes accessed | tf_op | source)
XLA Modules:
  0.0 19.7 jit_solution(7793772791041029329)
XLA Ops:
  0.0 18.1 %shard_map.64 = bf16[16,6144]{1,0:T(8,128)(2,1)} custom-call(bf16[2,4,16,384]{3,2,1,0:T(8,128)(2,1)} %latent_hbm.1, f32[384]{0:T(512)} %gain_hbm.1, f32[384]{0:T(512)} %bias1_hbm.1, f32[192]{0:T(256)} %bias2_hbm.1, bf16[27,96,384]{2,1,0:T(8,128)(2,1)} %w1_hbm.1, bf16[9,192,384]{2,1,0:T(8,128)(2,1)} %bitcast.3), custom_call_target="tpu_custom_call" | custom-call | flops 1698693120 | bytes 4194304 | tf_op jit(solution)/shard_map/pallas_call | solution.py:358
  18.1 1.6 %copy.8 = bf16[2,8,6144]{2,1,0:T(8,128)(2,1)} copy(bf16[2,8,6144]{2,1,0:T(8,128)(2,1)} %bitcast.2) | data formatting | bytes 393216

commit v10 on v5

--- a/solution.py
+++ b/solution.py
@@ -345,6 +345,19 @@
         for s in range(n_tm):
             up_copy(s).wait_send()
         row_copy(1, 1, rows + 1, above).wait_send()
+
+
+def deliver(held_hbm, out_hbm, sems):
+    count = sems.shape[0]
+    width = out_hbm.shape[1] // count
+    copies = []
+    for k in range(count):
+        part = pl.ds(k * width, width)
+        copies.append(pltpu.make_async_copy(held_hbm.at[:, part], out_hbm.at[:, part], sems.at[k]))
+    for copy in copies:
+        copy.start()
+    for copy in copies:
+        copy.wait()
 
 
 def local(n_tm, n_rows, latent, gain_first, conv_first, bias_first, conv_upper, bias_upper):
@@ -401,6 +414,13 @@
         conv_first,
         jnp.swapaxes(conv_upper, 1, 2),
     )
+    decoded = pl.pallas_call(
+        deliver,
+        out_shape=jax.ShapeDtypeStruct(decoded.shape, BF16),
+        in_specs=[hbm],
+        out_specs=hbm,
+        scratch_shapes=[dma((4,))],
+    )(decoded)
     return decoded.reshape(frames, 2 * rows, 2 * width * outputs)
 
 

time: 19.8 us -> 25.3 us (1.28)
  Pallas kernels: 18 us -> 25.1 us
  local copies, waits for them, and re-layouts: 1.62 us -> 0 us
    pallas_call x0 -> x1, Pallas kernels: none -> 7.09 us  [local(): pl.pallas_call(deliver, out_shape=jax.ShapeDtypeStruct(decoded.shape, BF1...]
    unnamed x1 -> x0, local copies, waits for them, and re-layouts: 1.62 us -> none
where the time goes in v10:
time: 25.3 us; the launch traced here: 25.1 us
  Pallas kernels  25.1 us (99%)
    pallas_call x1, Pallas kernels, local(): pl.pallas_call(functools.partial(kernel, n_tm, n_rows), out_shape=jax.Sha...  18 us
    pallas_call x1, Pallas kernels, local(): pl.pallas_call(deliver, out_shape=jax.ShapeDtypeStruct(decoded.shape, BF1...  7.09 us

profile of v10, /device:TPU:0, one launch (start us, length us, event | category | flops | bytes accessed | tf_op | source)
XLA Modules:
  0.0 25.1 jit_solution(3911662307027829226)
XLA Ops:
  0.0 18.0 %shard_map.64.held_hbm = bf16[16,6144]{1,0:T(8,128)(2,1)} custom-call(bf16[2,4,16,384]{3,2,1,0:T(8,128)(2,1)} %latent_hbm.1, f32[384]{0:T(512)} %gain_hbm.1, f32[384]{0:T(512)} %bias1_hbm.1, f32[192]{0:T(256)} %bias2_hbm.1, bf16[27,96,384]{2,1,0:T(8,128)(2,1)} %w1_hbm.1, bf16[9,192,384]{2,1,0:T(8,128)(2,1)} %bitcast.2), custom_call_target="tpu_custom_call" | custom-call | flops 1698693120 | bytes 4194304 | tf_op jit(solution)/shard_map/pallas_call | solution.py:374
  18.0 7.1 %shard_map.65 = bf16[16,6144]{1,0:T(8,128)(2,1)} custom-call(bf16[16,6144]{1,0:T(8,128)(2,1)} %shard_map.64.held_hbm), custom_call_target="tpu_custom_call" | custom-call | tf_op jit(solution)/shard_map/pallas_call | solution.py:417

commit v11 on v5

--- a/solution.py
+++ b/solution.py
@@ -117,18 +117,18 @@
     def up_copy(s):
         return act_copy(s, 2, pl.ds(0, 1), pl.ds(rows + 1, 1), above)
 
+    @pl.when(has_below)
+    def _():
+        for s in range(n_tm):
+            down_copy(s).start()
+
+    @pl.when(has_above)
+    def _():
+        for s in range(n_tm):
+            up_copy(s).start()
+
     for d in range(1, n_tm):
         main_copy(lax.rem(me + d, n_tm)).start()
-
-    @pl.when(has_below)
-    def _():
-        for s in range(n_tm):
-            down_copy(s).start()
-
-    @pl.when(has_above)
-    def _():
-        for s in range(n_tm):
-            up_copy(s).start()
 
     recv[mine, pl.ds(1, rows)] = send[me]
     all_frames = n_tm * frames

time: 19.8 us -> 19.8 us (level)
  no operation moved by 1% of the time
where the time goes in v11:
time: 19.8 us; the launch traced here: 19.7 us
  Pallas kernels  18 us (91%)
  local copies, waits for them, and re-layouts  1.62 us (8%)
    pallas_call x1, Pallas kernels, local(): pl.pallas_call(functools.partial(kernel, n_tm, n_rows), out_shape=jax.Sha...  18 us
    unnamed x1, local copies, waits for them, and re-layouts  1.62 us

profile of v11, /device:TPU:0, one launch (start us, length us, event | category | flops | bytes accessed | tf_op | source)
XLA Modules:
  0.0 19.7 jit_solution(8358039166639227460)
XLA Ops:
  0.0 18.0 %shard_map.64 = bf16[16,6144]{1,0:T(8,128)(2,1)} custom-call(bf16[2,4,16,384]{3,2,1,0:T(8,128)(2,1)} %latent_hbm.1, f32[384]{0:T(512)} %gain_hbm.1, f32[384]{0:T(512)} %bias1_hbm.1, f32[192]{0:T(256)} %bias2_hbm.1, bf16[27,96,384]{2,1,0:T(8,128)(2,1)} %w1_hbm.1, bf16[9,192,384]{2,1,0:T(8,128)(2,1)} %bitcast.3), custom_call_target="tpu_custom_call" | custom-call | flops 1698693120 | bytes 4194304 | tf_op jit(solution)/shard_map/pallas_call | solution.py:361
  18.0 1.6 %copy.8 = bf16[2,8,6144]{2,1,0:T(8,128)(2,1)} copy(bf16[2,8,6144]{2,1,0:T(8,128)(2,1)} %bitcast.2) | data formatting | bytes 393216

commit v12 on v8

--- a/solution.py
+++ b/solution.py
@@ -242,19 +242,16 @@
 
     for k in range(1, pairs + 1):
         pair = lax.rem(lax.div(me, 2) + k, pairs)
-        total = jnp.zeros((2 * cells, chans), F32)
+        windows = []
         for dt in range(3):
-            windows = []
             for dy in range(3):
                 for dx in range(3):
                     start = pair * (2 * frames) + dt
                     view = shifted[dx, pl.ds(start, 2 * frames), pl.ds(dy, rows)]
                     windows.append(view.reshape(2 * cells, LANES))
-            total = total + jnp.dot(
-                jnp.concatenate(windows, axis=1),
-                wpad[pl.ds(dt * 9 * LANES, 9 * LANES)],
-                preferred_element_type=F32,
-            )
+        total = jnp.dot(
+            jnp.concatenate(windows, axis=1), wpad[...], preferred_element_type=F32
+        )
         sums = total.reshape(2, frames, rows, width, chans)
         if k < pairs:
             for c in range(2):

time: 19.8 us -> 19.8 us (level)
  no operation moved by 1% of the time
where the time goes in v12:
time: 19.8 us; the launch traced here: 19.7 us
  Pallas kernels  18.1 us (91%)
  local copies, waits for them, and re-layouts  1.62 us (8%)
    pallas_call x1, Pallas kernels, local(): pl.pallas_call(functools.partial(kernel, n_tm, n_rows), out_shape=jax.Sha...  18.1 us
    unnamed x1, local copies, waits for them, and re-layouts  1.62 us

profile of v12, /device:TPU:0, one launch (start us, length us, event | category | flops | bytes accessed | tf_op | source)
XLA Modules:
  0.0 19.7 jit_solution(6543789169261202157)
XLA Ops:
  0.0 18.1 %shard_map.64 = bf16[16,6144]{1,0:T(8,128)(2,1)} custom-call(bf16[2,4,16,384]{3,2,1,0:T(8,128)(2,1)} %latent_hbm.1, f32[384]{0:T(512)} %gain_hbm.1, f32[384]{0:T(512)} %bias1_hbm.1, f32[192]{0:T(256)} %bias2_hbm.1, bf16[27,96,384]{2,1,0:T(8,128)(2,1)} %w1_hbm.1, bf16[9,192,384]{2,1,0:T(8,128)(2,1)} %bitcast.3), custom_call_target="tpu_custom_call" | custom-call | flops 1698693120 | bytes 4194304 | tf_op jit(solution)/shard_map/pallas_call | solution.py:370
  18.1 1.6 %copy.8 = bf16[2,8,6144]{2,1,0:T(8,128)(2,1)} copy(bf16[2,8,6144]{2,1,0:T(8,128)(2,1)} %bitcast.2) | data formatting | bytes 393216
